TPU v7x, 128 devices: a whole 4x4x4 slice. The times are simulated.
128 devices in a mesh: seq: 16 (over z, y), head: 8 (over x, core).
Axes of the slice: x: 4, y: 4, z: 4, core: 2. Of those that a mesh axis runs over, the one named last changes fastest.
Arguments:
- queries: bfloat16 [16384, 4096], P(('seq', 'head')), may hold values from -6 to 6
- keys: bfloat16 [16384, 2, 4096], P(('seq', 'head')), may hold values from -6 to 6
- values: bfloat16 [16384, 2, 4096], P(('seq', 'head')), may hold values from -6 to 6
- betas: bfloat16 [16384, 2, 16], P(('seq', 'head')), may hold values from 0.2 to 2, as said below
- gate: bfloat16 [16384, 4096], P(('seq', 'head')), may hold values from -6 to 6
- norm_gain: float32 [256], replicated, may hold values from 0.1 to 1.9
Outputs:
- mixed: bfloat16 [16384, 4096], P(('seq', 'head'))
Inputs may be any that keep to these rules, and one draw needn't show every extreme that they name: `betas`: each entry is the step size of one reflection of one head.
All inputs are finite; a program needn't handle non-finite values.
Results may differ from a plain program's by a relative error of at most 0.0049.
Values may be sent and summed in bfloat16 or wider, within the bound.
A program may use at most 128 MiB of HBM per device.

v0:
```python
import jax
import jax.numpy as jnp
from jax import lax
from jax.sharding import Mesh
from jax.sharding import PartitionSpec as P

REFL = 2
CT = 128
HEAD = ("head_0", "head_1")
SEQ = ("seq_0", "seq_1")
SEQ_HEAD = ("seq_0", "seq_1", "head_0", "head_1")


epsilon = 1e-06
highest = lax.Precision.HIGHEST


def in_blocks(array, dim, devices):
    before, after = (array.shape[:dim], array.shape[dim + 1 :])
    return jnp.moveaxis(array.reshape(*before, devices, -1, *after), dim, 0)


def in_order(blocks, dim):
    dims = list(blocks.shape[1:])
    dims[dim] *= blocks.shape[0]
    return jnp.moveaxis(blocks, 0, dim).reshape(dims)


def exchange_in_order(blocks, axes, turns):
    dims = [lax.axis_size(a) for a in axes]
    blocks = blocks.reshape(*dims, *blocks.shape[1:])
    for k in turns:
        blocks = lax.all_to_all(blocks, axes[k], split_axis=k, concat_axis=k, tiled=True)
    return blocks.reshape(-1, *blocks.shape[len(axes) :])


def one_axis_at_a_time(array, axes, turns, split_dim, concat_dim):
    blocks = in_blocks(array, split_dim, lax.axis_size(axes))
    return in_order(exchange_in_order(blocks, axes, turns), concat_dim)


def nothing_yet(array, identity):
    return jax.tree.map(
        lambda a, e: jnp.broadcast_to(jnp.asarray(e, a.dtype), a.shape), array, identity
    )


def entering(array, axes, combine, identity):
    before = start = nothing_yet(array, identity)
    subtotal = array
    for axis in reversed(axes):
        devices, here = (lax.axis_size(axis), lax.axis_index(axis))
        pieces = jax.tree.map(lambda part: lax.all_gather(part, axis), subtotal)
        inside, subtotal = (start, start)
        for k in range(devices):
            passed = k < here
            subtotal = combine(subtotal, jax.tree.map(lambda part: part[k], pieces))
            inside = jax.tree.map(lambda new, old: jnp.where(passed, new, old), subtotal, inside)
        before = combine(inside, before)
    return before


def two_step_exchange(array, groups, turns, split_dim, concat_dim):
    devices = lax.axis_size(groups[0]) * lax.axis_size(groups[1])
    blocks = in_blocks(array, split_dim, devices)
    return in_order(exchange_in_order(blocks, groups, turns), concat_dim)


def unit_rows(matrix):
    return matrix / jnp.sqrt(jnp.sum(matrix * matrix, axis=-1, keepdims=True) + epsilon)


def matmul_heads(left_side, right_side):
    return jnp.einsum("hde,hef->hdf", left_side, right_side, precision=highest)


def combine_pairs(earlier, later):
    return (matmul_heads(later[0], earlier[0]), matmul_heads(later[0], earlier[1]) + later[1])


def block_factors(key_parts, value_parts, beta_parts):
    seq_rows = key_parts.shape[0]
    local_heads = key_parts.shape[2]
    width_per_head = key_parts.shape[3]
    blocks = seq_rows // CT
    block_steps = CT * REFL
    k_unit = unit_rows(key_parts.astype(jnp.float32))
    k_blocks = (
        k_unit.reshape(blocks, CT, REFL, local_heads, width_per_head)
        .transpose(0, 3, 1, 2, 4)
        .reshape(blocks, local_heads, block_steps, width_per_head)
    )
    v_blocks = (
        value_parts.astype(jnp.float32)
        .reshape(blocks, CT, REFL, local_heads, width_per_head)
        .transpose(0, 3, 1, 2, 4)
        .reshape(blocks, local_heads, block_steps, width_per_head)
    )
    b_blocks = (
        beta_parts.astype(jnp.float32)
        .reshape(blocks, CT, REFL, local_heads)
        .transpose(0, 3, 1, 2)
        .reshape(blocks, local_heads, block_steps)
    )
    gram_rows = jnp.einsum("chid,chjd->chij", k_blocks, k_blocks, precision=highest)
    lower_part = jnp.tril(gram_rows, -1) * b_blocks[:, :, None, :]
    solved = lax.linalg.triangular_solve(
        lower_part,
        jnp.concatenate([k_blocks, v_blocks], axis=-1),
        left_side=True,
        lower=True,
        unit_diagonal=True,
    )
    w_rows = solved[..., :width_per_head] * b_blocks[..., None]
    y_rows = solved[..., width_per_head:] * b_blocks[..., None]
    identity = jnp.eye(width_per_head, dtype=jnp.float32)
    trans_a = identity - jnp.einsum("chid,chie->chde", k_blocks, w_rows, precision=highest)
    trans_b = jnp.einsum("chid,chie->chde", k_blocks, y_rows, precision=highest)
    return (k_blocks, w_rows, y_rows, trans_a, trans_b)


def shards(queries, keys, values, betas, gate, norm_gain):
    tok_rows = queries.shape[0]
    width_per_head = norm_gain.shape[0]
    head_count = queries.shape[1] // width_per_head
    query_parts = queries.reshape(tok_rows, 1, head_count, width_per_head)
    key_parts = keys.reshape(tok_rows, REFL, head_count, width_per_head)
    value_parts = values.reshape(tok_rows, REFL, head_count, width_per_head)
    beta_parts = betas.reshape(tok_rows, REFL, head_count, 1)
    key_parts, value_parts, beta_parts = (
        lax.all_to_all(key_parts, HEAD, split_axis=2, concat_axis=0, tiled=True),
        lax.all_to_all(value_parts, HEAD, split_axis=2, concat_axis=0, tiled=True),
        lax.all_to_all(beta_parts, HEAD, split_axis=2, concat_axis=0, tiled=True),
    )
    k_blocks, w_rows, y_rows, trans_a, trans_b = block_factors(key_parts, value_parts, beta_parts)
    query_parts = one_axis_at_a_time(query_parts, HEAD, (1, 0), 2, 0)
    seq_rows = key_parts.shape[0]
    local_heads = key_parts.shape[2]
    blocks = seq_rows // CT
    block_steps = CT * REFL
    identity_heads = jnp.broadcast_to(
        jnp.eye(width_per_head, dtype=jnp.float32), (local_heads, width_per_head, width_per_head)
    )
    zero_heads = jnp.zeros((local_heads, width_per_head, width_per_head), jnp.float32)

    def compose(carried_pair, pieces):
        return (combine_pairs(carried_pair, pieces), None)

    device_pair, unused_rows = lax.scan(compose, (identity_heads, zero_heads), (trans_a, trans_b))
    device_a, device_b = device_pair
    prefix_a, prefix_b = entering(
        (device_a, device_b), SEQ, combine_pairs, (identity_heads, zero_heads)
    )
    query_blocks = (
        unit_rows(query_parts[:, 0].astype(jnp.float32))
        .reshape(blocks, CT, local_heads, width_per_head)
        .transpose(0, 2, 1, 3)
    )
    step_iota = lax.broadcasted_iota(jnp.int32, (CT, block_steps), 1)
    token_iota = lax.broadcasted_iota(jnp.int32, (CT, block_steps), 0)
    causal = step_iota // REFL <= token_iota
    scores = jnp.where(
        causal,
        jnp.einsum("chtd,chid->chti", query_blocks, k_blocks, precision=highest),
        jnp.zeros((), jnp.float32),
    )

    def advance(carried, pieces):
        w_now, y_now, k_now, q_now, score_now = pieces
        update_rows = y_now - jnp.einsum("hid,hde->hie", w_now, carried, precision=highest)
        output = jnp.einsum("htd,hde->hte", q_now, carried, precision=highest) + jnp.einsum(
            "hti,hie->hte", score_now, update_rows, precision=highest
        )
        carried = carried + jnp.einsum("hid,hie->hde", k_now, update_rows, precision=highest)
        return (carried, output)

    final_state, outputs = lax.scan(
        advance, prefix_b, (w_rows, y_rows, k_blocks, query_blocks, scores)
    )
    outputs = outputs.transpose(0, 2, 1, 3).reshape(seq_rows, local_heads, width_per_head)
    normed = (
        outputs
        * lax.rsqrt(jnp.mean(outputs * outputs, axis=-1, keepdims=True) + epsilon)
        * norm_gain
    ).astype(jnp.bfloat16)
    normed = two_step_exchange(normed, ("head_0", "head_1"), (1, 0), 0, 1)
    gated = normed.astype(jnp.float32).reshape(tok_rows, head_count * width_per_head) * jax.nn.silu(
        gate.astype(jnp.float32)
    )
    return gated.astype(jnp.bfloat16)


def solution(mesh):
    torus = Mesh(mesh.devices.reshape(4, 4, 4, 2), ("seq_0", "seq_1", "head_0", "head_1"))
    placed = (
        P(SEQ_HEAD, None),
        P(SEQ_HEAD, None, None),
        P(SEQ_HEAD, None, None),
        P(SEQ_HEAD, None, None),
        P(SEQ_HEAD, None),
        P(),
    )
    return jax.shard_map(
        shards, mesh=torus, in_specs=placed, out_specs=P(SEQ_HEAD, None), check_vma=False
    )
```

profile of v0, /device:TPU:96, one launch (start us, length us, event | category | flops | bytes accessed | tf_op | source)
XLA Modules:
  0.0 729.9 jit_solution(6590392618622536062)
XLA Ops:
  7.8 4.3 all-to-all-start.1
  12.1 4.9 copy.121
  17.0 3.8 copy.122
  20.8 4.8 all-to-all-start
  25.6 6.2 copy.130
  31.8 6.2 copy.131
  38.5 14.4 %all-to-all-done = bf16[128,2,16,256]{3,1,0,2:T(2,128)(2,1)S(1)} async-done(((bf16[128,2,16,256]{3,1,0,2:T(2,128)(2,1)}), bf16[128,2,16,256]{3,1,0,2:T(2,128)(2,1)S(1)}, u32[]{:S(2)}, u32[]{:S(2)}) %all-to-all-start) | async-done | bytes 2097184 | tf_op jit(solution)/shard_map/all_to_all | solution.py:131
  52.8 4.4 all-to-all-start.2
  57.2 3.3 multiply_reduce_fusion
  65.2 4.0 broadcast_divide_fusion
  69.2 6.1 reshape.120
  75.3 4.7 constant_dynamic-update-slice_fusion.1
  80.0 4.4 all-to-all-done.2
  84.4 5.3 convert_bitcast_fusion
  89.7 6.1 reshape.153
  95.8 10.2 %select_add_fusion = f32[8,2,256,256]{3,2,1,0:T(8,128)} fusion(f32[8,2,256,256]{3,2,1,0:T(8,128)} %reshape.120, f32[256,256]{1,0:T(8,128)S(1)} %get-tuple-element.199, f32[8,2,256]{2,1,0:T(2,128)S(1)} %copy.128, pred[256,256]{1,0:T(8,128)(4,1)S(1)} %get-tuple-element.198), kind=kOutput, calls=%fused_computation.43 | convolution fusion | flops 3225419776 | bytes 8732672 | tf_op jit(solution)/shard_map/chid,chjd->chij/dot_general | solution.py:105
  106.1 9.3 %while.30 = (s32[]{:T(128)}, f32[8,2,256,256]{3,2,1,0:T(8,128)}, s32[2,2]{1,0:T(2,128)S(1)}, f32[2,8,2,128,128]{4,3,0,2,1:T(8,128)}) while((s32[]{:T(128)}, f32[8,2,256,256]{3,2,1,0:T(8,128)}, s32[2,2]{1,0:T(2,128)S(1)}, f32[2,8,2,128,128]{4,3,0,2,1:T(8,128)}) %tuple.69), condition=%wide.while_cond.clone, body=%wide.while_body.sunk.clone | while | flops 2 | bytes 2098277 | solution.py:107
  106.7 4.2 bitcast_dynamic-update-slice_fusion.3
  111.5 3.9 bitcast_dynamic-update-slice_fusion.3
  115.4 315.2 %custom-call.3 = f32[8,2,2,128,128]{3,4,2,1,0:T(8,128)S(1)} custom-call(f32[8,2,2,128,128]{4,3,2,1,0:T(8,128)} %bitcast.190), custom_call_target="InvertDiagBlocksLowerTriangular" | custom-call | tf_op jit(solution)/shard_map/triangular_solve | solution.py:107
  430.6 4.7 constant_dynamic-update-slice_fusion
  435.3 6.1 fusion.30
  441.4 5.5 fusion.39
  447.0 4.1 fusion.29
  451.9 2.6 copy-done
  454.4 8.7 %fusion.74 = f32[8,2,256,256]{3,2,1,0:T(8,128)} fusion(f32[8,2,256,256]{3,2,1,0:T(8,128)S(1)} %copy-done, f32[8,2,256,256]{3,2,1,0:T(8,128)S(1)} %get-tuple-element.385), kind=kOutput, calls=%fused_computation.125 | convolution fusion | flops 3221225472 | bytes 12582912 | tf_op jit(solution)/shard_map/chid,chie->chde/dot_general | solution.py:118
  463.1 8.5 %convolution_subtract_fusion.1 = f32[8,2,256,256]{3,2,1,0:T(8,128)} fusion(f32[8,2,256,256]{3,2,1,0:T(8,128)S(1)} %copy-done, f32[8,2,256,256]{3,2,1,0:T(8,128)S(1)} %get-tuple-element.386, f32[256,256]{1,0:T(8,128)S(1)} %fusion.57), kind=kOutput, calls=%fused_computation.47 | convolution fusion | flops 3222274048 | bytes 12845056 | tf_op jit(solution)/shard_map/chid,chie->chde/dot_general | solution.py:117
  471.7 29.5 %while.31 = (s32[]{:T(128)}, f32[2,256,256]{2,1,0:T(8,128)S(1)}, f32[2,256,256]{2,1,0:T(8,128)S(1)}, f32[8,2,256,256]{3,2,1,0:T(8,128)}, f32[8,2,256,256]{3,2,1,0:T(8,128)}) while((s32[]{:T(128)}, f32[2,256,256]{2,1,0:T(8,128)S(1)}, f32[2,256,256]{2,1,0:T(8,128)S(1)}, f32[8,2,256,256]{3,2,1,0:T(8,128)}, ...), condition=%wide.region_2.3_spmd.clone.clone, body=%wide.region_1.2_spmd.clone.sunk.clone | while | flops 805568512 | bytes 5768786 | solution.py:149
  473.5 1.9 convolution_add_fusion.17
  480.9 1.9 convolution_add_fusion.17
  484.6 1.9 convolution_add_fusion.17
  499.3 1.9 convolution_add_fusion.17
  502.8 29.6 %all-gather.9.cloned.1.call-done = f32[8,256,256]{2,1,0:T(8,128)} async-done(((f32[2,256,256]{2,1,0:T(8,128)}), f32[8,256,256]{2,1,0:T(8,128)}) %all-gather.9.cloned.1.call-update) | async-done | bytes 2097168 | tf_op jit(solution)/shard_map/all_gather | solution.py:53
  538.8 26.2 %all-gather.13.cloned.1.call-done = f32[8,256,256]{2,1,0:T(8,128)} async-done(((f32[2,256,256]{2,1,0:T(8,128)}), f32[8,256,256]{2,1,0:T(8,128)}) %all-gather.13.cloned.1.call-update) | async-done | bytes 2097168 | tf_op jit(solution)/shard_map/all_gather | solution.py:53
  572.6 4.6 all_to_all.47
  578.2 4.5 all-to-all-start.4
  582.8 15.3 %all-to-all-done.4 = bf16[4,2,128,1,2,256]{5,2,4,1,3,0:T(8,128)(2,1)S(1)} async-done(((bf16[4,2,128,1,2,256]{5,2,4,1,3,0:T(8,128)(2,1)}), bf16[4,2,128,1,2,256]{5,2,4,1,3,0:T(8,128)(2,1)S(1)}, u32[]{:S(2)}, u32[]{:S(2)}) %all-to-all-start.4) | async-done | bytes 1048608 | tf_op jit(solution)/shard_map/all_to_all | solution.py:33
  599.0 2.2 bitcast_divide_fusion
  601.3 5.6 convolution_select_fusion
  608.4 19.7 %all-gather.15.cloned.1.call-done = f32[8,256,256]{2,1,0:T(8,128)} async-done(((f32[2,256,256]{2,1,0:T(8,128)}), f32[8,256,256]{2,1,0:T(8,128)}) %all-gather.15.cloned.1.call-update) | async-done | bytes 2097168 | tf_op jit(solution)/shard_map/all_gather | solution.py:53
  628.1 1.9 convolution_add_fusion.10
  634.8 53.0 %while.29 = (s32[]{:T(128)}, f32[2,256,256]{2,1,0:T(8,128)S(1)}, f32[8,2,128,256]{3,2,1,0:T(8,128)}, f32[8,2,256,256]{3,2,1,0:T(8,128)}, f32[8,2,256,256]{3,2,1,...) while((s32[]{:T(128)}, f32[2,256,256]{2,1,0:T(8,128)S(1)}, ...), condition=%wide.region_5.6_spmd.clone, body=%wide.region_4.5_spmd.sunk.clone | while | flops 1208287232 | bytes 6555749 | solution.py:177
  637.1 2.2 convolution_add_fusion.16
  639.3 2.1 fusion.156
  643.7 2.2 convolution_add_fusion.16
  645.9 2.1 fusion.156
  650.3 2.2 convolution_add_fusion.16
  652.5 2.1 fusion.156
  656.9 2.2 convolution_add_fusion.16
  659.1 2.1 fusion.156
  663.5 2.2 convolution_add_fusion.16
  665.7 2.1 fusion.156
  670.1 2.2 convolution_add_fusion.16
  672.3 2.1 fusion.156
  676.7 2.2 convolution_add_fusion.16
  678.9 2.1 fusion.156
  683.3 2.2 convolution_add_fusion.16
  685.5 2.1 fusion.156
  687.8 2.1 fusion.36
  690.5 4.6 all_to_all.48
  696.1 4.2 all-to-all-start.6
  701.0 14.7 %all-to-all-done.6 = bf16[4,2,128,2,256]{4,2,3,1,0:T(8,128)(2,1)S(1)} async-done(((bf16[4,2,128,2,256]{4,2,3,1,0:T(8,128)(2,1)}), bf16[4,2,128,2,256]{4,2,3,1,0:T(8,128)(2,1)S(1)}, u32[]{:S(2)}, u32[]{:S(2)}) %all-to-all-start.6) | async-done | bytes 1048608 | tf_op jit(solution)/shard_map/all_to_all | solution.py:33
  717.3 1.9 copy.146
  720.8 2.3 copy.148
  (165 shorter events, 77.5 us)
Async XLA Ops:
  7.8 13.0 %all-to-all-start.1 = ((bf16[128,2,16,1]{0,1,3,2:T(2,128)(2,1)}), bf16[128,2,16,1]{0,1,3,2:T(2,128)(2,1)S(1)}, u32[]{:S(2)}, u32[]{:S(2)}) async-start(bf16[128,2,16,1]{0,1,3,2:T(2,128)(2,1)} %bitcast.125), calls=%async_computation.1 | async-start | bytes 16384 | tf_op jit(solution)/shard_map/all_to_all | solution.py:133
  20.8 32.0 %all-to-all-start = ((bf16[128,2,16,256]{3,1,0,2:T(2,128)(2,1)}), bf16[128,2,16,256]{3,1,0,2:T(2,128)(2,1)S(1)}, u32[]{:S(2)}, u32[]{:S(2)}) async-start(bf16[128,2,16,256]{3,1,0,2:T(2,128)(2,1)} %copy.122), calls=%async_computation | async-start | bytes 4194304 | tf_op jit(solution)/shard_map/all_to_all | solution.py:131
  52.8 31.6 %all-to-all-start.2 = ((bf16[128,2,16,256]{3,1,0,2:T(2,128)(2,1)}), bf16[128,2,16,256]{3,1,0,2:T(2,128)(2,1)}, u32[]{:S(2)}, u32[]{:S(2)}) async-start(bf16[128,2,16,256]{3,1,0,2:T(2,128)(2,1)} %copy.131), calls=%async_computation.2 | async-start | bytes 4194304 | tf_op jit(solution)/shard_map/all_to_all | solution.py:132
  57.2 475.2 %all-gather.9.cloned.1.call-start = ((), (), s32[]{:S(2)}) async-start(), calls=%async_computation.7 | async-start | bytes 2621440 | tf_op jit(solution)/shard_map/all_gather | solution.py:53
  63.4 1.8 copy-start.22
  435.3 11.6 %slice-start = ((s8[8388608]{0:T(1024)(128)(4,1)}), s8[4194304]{0:T(1024)(128)(4,1)S(1)}, s32[]{:S(2)}) async-start(s8[8388608]{0:T(1024)(128)(4,1)} %bitcast.177), calls=%async_computation.11 | async-start | bytes 8388608
  441.4 5.6 slice-start.1
  451.1 3.3 copy-start
  451.9 11.3 %copy-start.3 = (f32[8,2,256,256]{3,2,1,0:T(8,128)}, f32[8,2,256,256]{3,2,1,0:T(8,128)S(1)}, u32[]{:S(2)}) copy-start(f32[8,2,256,256]{3,2,1,0:T(8,128)S(1)} %get-tuple-element.385) | copy-start | bytes 12582916
  451.9 11.3 %copy-start.4 = (f32[8,2,256,256]{3,2,1,0:T(8,128)}, f32[8,2,256,256]{3,2,1,0:T(8,128)S(1)}, u32[]{:S(2)}) copy-start(f32[8,2,256,256]{3,2,1,0:T(8,128)S(1)} %get-tuple-element.386) | copy-start | bytes 12582916
  501.2 0.8 copy-start.5
  501.2 1.0 copy-start.6
  502.0 63.0 %all-gather.13.cloned.1.call-start = ((), (), s32[]{:S(2)}) async-start(), calls=%async_computation.9 | async-start | bytes 2621440 | tf_op jit(solution)/shard_map/all_gather | solution.py:53
  502.8 105.6 %all-gather.11.cloned.1.call-start = ((), (), s32[]{:S(2)}) async-start(), calls=%async_computation.8 | async-start | bytes 2621440 | tf_op jit(solution)/shard_map/all_gather | solution.py:53
  532.4 1.8 copy-start.2
  534.3 2.1 copy-start.16
  534.9 0.8 copy-start.18
  536.4 0.8 copy-start.20
  538.7 89.3 %all-gather.15.cloned.1.call-start = ((), (), s32[]{:S(2)}) async-start(), calls=%async_computation.10 | async-start | bytes 2621440 | tf_op jit(solution)/shard_map/all_gather | solution.py:53
  565.0 1.8 copy-start.25
  567.4 3.0 copy-start.12
  568.1 0.8 copy-start.14
  578.2 19.8 %all-to-all-start.4 = ((bf16[4,2,128,1,2,256]{5,2,4,1,3,0:T(8,128)(2,1)}), bf16[4,2,128,1,2,256]{5,2,4,1,3,0:T(8,128)(2,1)S(1)}, u32[]{:S(2)}, u32[]{:S(2)}) async-start(bf16[4,2,128,1,2,256]{5,2,4,1,3,0:T(8,128)(2,1)} %copy.140), calls=%async_computation.4 | async-start | bytes 2097152 | tf_op jit(solution)/shard_map/all_to_all | solution.py:33
  598.0 1.0 copy-start.8
  598.1 3.2 copy-start.1
  601.3 5.6 copy-start.11
  601.3 5.6 copy-start.17
  601.3 5.6 copy-start.19
  601.3 5.6 copy-start.21
  628.1 1.9 copy-start.7
  628.1 3.6 copy-start.24
  632.4 1.0 copy-start.23
  632.4 1.7 copy-start.10
  632.4 1.7 copy-start.13
  632.4 1.7 copy-start.15
  687.8 2.2 copy-start.9
  687.8 2.2 copy-start.27
  695.0 5.3 copy-start.26
  696.1 19.6 %all-to-all-start.6 = ((bf16[4,2,128,2,256]{4,2,3,1,0:T(8,128)(2,1)}), bf16[4,2,128,2,256]{4,2,3,1,0:T(8,128)(2,1)S(1)}, u32[]{:S(2)}, u32[]{:S(2)}) async-start(bf16[4,2,128,2,256]{4,2,3,1,0:T(8,128)(2,1)} %copy.145), calls=%async_computation.6 | async-start | bytes 2097152 | tf_op jit(solution)/shard_map/all_to_all | solution.py:33
Sparse Core Ops, SparseCore 0:
  502.1 30.2 all-gather.8
  534.1 30.8 all-gather.12
  566.7 28.8 all-gather.10
  597.1 30.9 all-gather.14
where the time goes:
time: 741 us; the launch traced here: 730 us
  other arithmetic  339 us (46%)
  matrix products  147 us (20%)
  waiting for transfers between devices  125 us (17%)
  local copies, waits for them, and re-layouts  73.2 us (10%)
  starting transfers between devices  22.3 us (3%)
  between operations  14.1 us (2%)
  blocking collectives  9.15 us (1%)
    another operation x4, other arithmetic, block_factors(): lax.linalg.triangular_solve(lower_part, jnp.concatenate([k_blocks, v_bloc...  315 us
    all_gather x4, waiting for transfers between devices, entering(): pieces = jax.tree.map(lambda part: lax.all_gather(part, axis), subtotal)  75.5 us
    dot_general x31, matrix products, matmul_heads(): return jnp.einsum('hde,hef->hdf', left_side, right_side, precision=highest)  45.4 us
    all_to_all x2, waiting for transfers between devices, exchange_in_order(): lax.all_to_all(blocks, axes[k], split_axis=k, concat_axis=k, tiled=True)  30 us
    unnamed x66, local copies, waits for them, and re-layouts  26.3 us
    dot_general x8, matrix products, advance(): jnp.einsum('hid,hie->hde', k_now, update_rows, precision=highest)  17.3 us
    dot_general x8, matrix products, advance(): jnp.einsum('hti,hie->hte', score_now, update_rows, precision=highest)  16.8 us
    another operation x3, matrix products, block_factors(): lax.linalg.triangular_solve(lower_part, jnp.concatenate([k_blocks, v_bloc...  15.7 us
  transfers between devices with their start and end apart: 9, of which 7 were waited for; matrix products, arithmetic and copies ran while one was open for 9% of the time, Pallas kernels for 0%

commit v1 on v0

v1 whole, which is shorter than its diff:
```python
import functools

import jax
import jax.numpy as jnp
from jax import lax
from jax.experimental import pallas as pl
from jax.experimental.pallas import tpu as pltpu
from jax.sharding import Mesh
from jax.sharding import PartitionSpec as P

H = 16
DK = 256
CT = 128
STEPS = 256
EPS = 1e-06
LEVELS = 8
PER = 2
f32 = jnp.float32
bf16 = jnp.bfloat16
AXES = ("z", "y", "x", "core")
highest = lax.Precision.HIGHEST


def mm(a, b, dims=((1,), (0,))):
    return lax.dot_general(a, b, (dims, ((), ())), preferred_element_type=f32)


def split(x):
    hi = x.astype(bf16)
    return hi, (x - hi.astype(f32)).astype(bf16)


def mm_right(a, b):
    hi, lo = b
    return mm(a, hi) + mm(a, lo)


def mm_both(a, b):
    return mm(a[0], b[0]) + (mm(a[0], b[1]) + mm(a[1], b[0]))


def factors(k, v, q, beta_row, mask_ref):
    row = lax.broadcasted_iota(jnp.int32, (STEPS, STEPS), 0)
    col = lax.broadcasted_iota(jnp.int32, (STEPS, STEPS), 1)
    eye = row == col
    gram = mm(k, k, ((1,), (1,)))
    g = jnp.sum(jnp.where(eye, gram, 0.0), axis=0, keepdims=True) + EPS
    c = beta_row / g
    lower = jnp.where(row > col, gram, 0.0)
    low = split(lower)
    tau = jnp.where(eye, c, 0.0)
    for level in range(LEVELS):
        edge = low[0] * mask_ref[level]
        tb = tau.astype(bf16)
        step = (edge.astype(f32) * c if level == 0 else mm(edge, tb)).astype(bf16)
        tau = tau - mm(tb, step)
    tb = tau.astype(bf16)
    t32 = tb.astype(f32)
    rest = jnp.where(eye, 1.0, 0.0) - t32 * (g / beta_row) - mm_right(tb, low)
    tau = t32 + mm(rest.astype(bf16), tb)
    ts = split(tau)
    w = split(mm(ts[0], k) + mm(ts[1], k))
    ts = split(tau * jnp.sqrt(g))
    y = split(mm(ts[0], v) + mm(ts[1], v))
    kt = k.T
    a = jnp.where(eye, 1.0, 0.0) - mm_right(kt, w)
    b = mm_right(kt, y)
    token = lax.broadcasted_iota(jnp.int32, (CT, STEPS), 0)
    step_of = lax.broadcasted_iota(jnp.int32, (CT, STEPS), 1)
    p = split(jnp.where(step_of // 2 <= token, mm(q, k, ((1,), (1,))), 0.0))
    q32 = q.astype(f32)
    unit = lax.rsqrt(jnp.sum(q32 * q32, axis=-1, keepdims=True) + EPS)
    qt = (q32 - mm_both(p, w)) * unit
    ot = mm_both(p, y) * unit
    return a, b, qt, ot


def make_masks(mask_ref):
    row = lax.broadcasted_iota(jnp.int32, (STEPS, STEPS), 0)
    col = lax.broadcasted_iota(jnp.int32, (STEPS, STEPS), 1)
    differ = jnp.bitwise_xor(row, col)
    for level in range(LEVELS):
        inside = (differ >= (1 << level)) & (differ < (2 << level))
        mask_ref[level] = jnp.where(inside, 1.0, 0.0).astype(bf16)


def local_kernel(q_ref, k_ref, v_ref, beta_ref, a_ref, b_ref, qt_ref, ot_ref, mask_ref):
    @pl.when(pl.program_id(0) == 0)
    def _():
        make_masks(mask_ref)

    for i in range(PER):
        lanes = slice(i * DK, (i + 1) * DK)
        k = k_ref[:, :, lanes].reshape(STEPS, DK)
        v = v_ref[:, :, lanes].reshape(STEPS, DK)
        a, b, qt, ot = factors(k, v, q_ref[:, lanes], beta_ref[i], mask_ref)
        a_ref[i] = a
        b_ref[i] = b
        qt_ref[i] = qt
        ot_ref[i] = ot


def local_factors(queries, keys, values, beta_rows):
    tokens = pl.BlockSpec((CT, PER * DK), lambda i: (0, i))
    pairs = pl.BlockSpec((CT, 2, PER * DK), lambda i: (0, 0, i))
    square = pl.BlockSpec((PER, DK, DK), lambda i: (i, 0, 0))
    half = pl.BlockSpec((PER, CT, DK), lambda i: (i, 0, 0))
    return pl.pallas_call(
        local_kernel,
        grid=(H // PER,),
        in_specs=[tokens, pairs, pairs, pl.BlockSpec((PER, 1, STEPS), lambda i: (i, 0, 0))],
        out_specs=[square, square, half, half],
        out_shape=[jax.ShapeDtypeStruct((H, DK, DK), f32)] * 2
        + [jax.ShapeDtypeStruct((H, CT, DK), f32)] * 2,
        scratch_shapes=[pltpu.VMEM((LEVELS, STEPS, STEPS), bf16)],
        compiler_params=pltpu.CompilerParams(vmem_limit_bytes=48 << 20),
    )(queries, keys, values, beta_rows)


def gated(o, gain, gate):
    scale = lax.rsqrt(jnp.mean(o * o, axis=-1, keepdims=True) + EPS)
    normed = (o * scale * gain).astype(bf16).astype(f32)
    gate = gate.astype(f32)
    return (normed * (gate / (1.0 + jnp.exp(-gate)))).astype(bf16)


def output_kernel(s_ref, qt_ref, ot_ref, gate_ref, gain_ref, out_ref):
    for i in range(PER):
        lanes = slice(i * DK, (i + 1) * DK)
        o = mm_both(split(qt_ref[i]), split(s_ref[i])) + ot_ref[i]
        out_ref[:, lanes] = gated(o, gain_ref[...], gate_ref[:, lanes])


def outputs(state, qt, ot, gate, gain):
    tokens = pl.BlockSpec((CT, PER * DK), lambda i: (0, i))
    square = pl.BlockSpec((PER, DK, DK), lambda i: (i, 0, 0))
    half = pl.BlockSpec((PER, CT, DK), lambda i: (i, 0, 0))
    return pl.pallas_call(
        output_kernel,
        grid=(H // PER,),
        in_specs=[square, half, half, tokens, pl.BlockSpec((1, DK), lambda i: (0, 0))],
        out_specs=tokens,
        out_shape=jax.ShapeDtypeStruct((CT, H * DK), bf16),
        compiler_params=pltpu.CompilerParams(vmem_limit_bytes=48 << 20),
    )(state, qt, ot, gate, gain)


def einmul(a, b):
    return jnp.einsum("hde,hef->hdf", a, b, precision=highest)


def prefixes(a, b):
    pairs = [(a[0], b[0])]
    for i in range(1, a.shape[0]):
        pairs.append((einmul(a[i], pairs[-1][0]), einmul(a[i], pairs[-1][1]) + b[i]))
    return pairs


def entering(start, pairs, index, stack=False):
    states = [start] + [einmul(p[0], start) + p[1] for p in pairs[:-1]]
    states = jnp.stack(states)
    if stack:
        return states
    return lax.dynamic_index_in_dim(states, index, 0, keepdims=False)


def shards(queries, keys, values, betas, gate, norm_gain):
    beta_rows = betas.astype(f32).transpose(2, 0, 1).reshape(H, 1, STEPS)
    a, b, qt, ot = local_factors(queries, keys, values, beta_rows)
    ab = jnp.concatenate([a, b], axis=-1).reshape(2, 4, 2, DK, 2 * DK)
    ab = lax.all_to_all(ab, "core", 0, 0, tiled=True)
    own = [(ab[i, ..., :DK].reshape(8, DK, DK), ab[i, ..., DK:].reshape(8, DK, DK)) for i in (0, 1)]
    chip_a = einmul(own[1][0], own[0][0])
    chip_b = einmul(own[1][0], own[0][1]) + own[1][1]
    ab = jnp.concatenate([chip_a, chip_b], axis=-1).reshape(4, 2, DK, 2 * DK)
    ab = lax.all_to_all(ab, "x", 0, 0, tiled=True)
    in_x = prefixes(ab[..., :DK], ab[..., DK:])
    ab = lax.all_gather(jnp.concatenate(in_x[-1], axis=-1), "y")
    in_y = prefixes(ab[..., :DK], ab[..., DK:])
    ab = lax.all_gather(jnp.concatenate(in_y[-1], axis=-1), "z")
    in_z = [(ab[i, ..., :DK], ab[i, ..., DK:]) for i in range(4)]
    state = jnp.zeros((2, DK, DK), f32)
    states = [state]
    for i in range(3):
        state = einmul(in_z[i][0], state) + in_z[i][1]
        states.append(state)
    state = lax.dynamic_index_in_dim(jnp.stack(states), lax.axis_index("z"), 0, keepdims=False)
    state = entering(state, in_y, lax.axis_index("y"))
    states = entering(state, in_x, 0, stack=True)
    states = lax.all_to_all(states, "x", 0, 0, tiled=True).reshape(8, DK, DK)
    later = einmul(own[0][0], states) + own[0][1]
    states = lax.all_to_all(jnp.stack([states, later]), "core", 0, 0, tiled=True)
    return outputs(states.reshape(H, DK, DK), qt, ot, gate, norm_gain.reshape(1, DK))


def solution(mesh):
    torus = Mesh(mesh.devices.reshape(4, 4, 4, 2), AXES)
    placed = (P(AXES, None), P(AXES, None, None), P(AXES, None, None), P(AXES, None, None), P(AXES, None), P())
    return jax.shard_map(
        shards, mesh=torus, in_specs=placed, out_specs=P(AXES, None), check_vma=False
    )
```

time: 741 us -> 378 us (0.51)
  other arithmetic: 339 us -> 14.9 us
  matrix products: 147 us -> 44.3 us
  Pallas kernels: 0 us -> 74.6 us
  blocking collectives: 9.15 us -> 72.1 us
  local copies, waits for them, and re-layouts: 73.2 us -> 29.9 us
  starting transfers between devices: 22.3 us -> 5 us
  waiting for transfers between devices: 125 us -> 117 us
    another operation x4, other arithmetic: 315 us -> 5.2 us  [the longest x1 2.67 us: shards(): jnp.stack([states, later])]
    dot_general x67 -> x24, matrix products: 131 us -> 44.3 us  [einmul(): return jnp.einsum('hde,hef->hdf', a, b, precision=highest)]
    pallas_call x0 -> x2, Pallas kernels: none -> 74.6 us  [the longest x1 67.2 us: local_factors(): pl.pallas_call(local_kernel, grid=(H // PER,), in_specs=[tokens, pairs, p...]
    all_to_all x2 -> x3, blocking collectives: 9.15 us -> 72.1 us  [the longest x1 53.5 us: shards(): ab = lax.all_to_all(ab, 'x', 0, 0, tiled=True)]
    all_to_all x5 -> x1, waiting for transfers between devices: 48.8 us -> 23.6 us  [shards(): states = lax.all_to_all(states, 'x', 0, 0, tiled=True).reshape(8, DK, DK)]
    unnamed x66 -> x42, local copies, waits for them, and re-layouts: 26.3 us -> 6.15 us
    all_gather x4 -> x2, waiting for transfers between devices: 75.5 us -> 93.8 us  [the longest x1 47.6 us: shards(): ab = lax.all_gather(jnp.concatenate(in_x[-1], axis=-1), 'y')]
    all_to_all x5 -> x1, starting transfers between devices: 22.1 us -> 4.74 us  [shards(): states = lax.all_to_all(states, 'x', 0, 0, tiled=True).reshape(8, DK, DK)]
  transfers between devices with their start and end apart: 9 -> 3, of which waited for: 7 -> 3; matrix products, arithmetic and copies ran while one was open for 9% -> 1% of each run, Pallas kernels for 0% -> 0%
where the time goes in v1:
time: 378 us; the launch traced here: 372 us
  waiting for transfers between devices  117 us (31%)
  Pallas kernels  74.6 us (20%)
  blocking collectives  72.1 us (19%)
  matrix products  44.3 us (12%)
  local copies, waits for them, and re-layouts  29.9 us (8%)
  other arithmetic  14.9 us (4%)
  between operations  13.8 us (4%)
  starting transfers between devices  5 us (1%)
    pallas_call x1, Pallas kernels, local_factors(): pl.pallas_call(local_kernel, grid=(H // PER,), in_specs=[tokens, pairs, p...  67.2 us
    all_to_all x1, blocking collectives, shards(): ab = lax.all_to_all(ab, 'x', 0, 0, tiled=True)  53.5 us
    all_gather x1, waiting for transfers between devices, shards(): ab = lax.all_gather(jnp.concatenate(in_x[-1], axis=-1), 'y')  47.6 us
    all_gather x1, waiting for transfers between devices, shards(): ab = lax.all_gather(jnp.concatenate(in_y[-1], axis=-1), 'z')  46.2 us
    dot_general x24, matrix products, einmul(): return jnp.einsum('hde,hef->hdf', a, b, precision=highest)  44.3 us
    all_to_all x1, waiting for transfers between devices, shards(): states = lax.all_to_all(states, 'x', 0, 0, tiled=True).reshape(8, DK, DK)  23.6 us
    all_to_all x1, blocking collectives, shards(): ab = lax.all_to_all(ab, 'core', 0, 0, tiled=True)  10.5 us
    all_to_all x1, blocking collectives, shards(): lax.all_to_all(jnp.stack([states, later]), 'core', 0, 0, tiled=True)  8.18 us
  transfers between devices with their start and end apart: 3, of which 3 were waited for; matrix products, arithmetic and copies ran while one was open for 1% of the time, Pallas kernels for 0%

profile of v1, /device:TPU:96, one launch (start us, length us, event | category | flops | bytes accessed | tf_op | source)
XLA Modules:
  0.0 372.2 jit_solution(7931498537364129753)
XLA Ops:
  6.5 0.7 convert_bitcast_fusion
  7.2 0.1 copy.42
  7.4 0.1 copy.43.beta_ref
  7.4 1.2 copy-done.2
  8.7 67.2 %shard_map.64 = (f32[16,256,256]{2,1,0:T(8,128)}, f32[16,256,256]{2,1,0:T(8,128)}, f32[16,128,256]{2,1,0:T(8,128)S(1)}, f32[16,128,256]{2,1,0:T(8,128)S(1)}) custom-call(bf16[128,4096]{1,0:T(8,128)(2,1)S(1)} %copy-done.2, bf16[128,2,4096]{2,1,0:T(2,128)(2,1)} %k_ref.1, bf16[128,2,4096]{2,1,0:T(2,128)(2,1)} %v_ref.1, f32[16,1,256]{2,1,0:T(1,128)S(1)} %copy.43.beta_ref), custom_call_target="tpu_custom_call" | custom-call | tf_op jit(solution)/shard_map/pallas_call | solution.py:108
  75.8 1.3 copy-done
  77.2 4.5 %pad_maximum_fusion = f32[16,256,512]{2,1,0:T(8,128)S(1)} fusion(f32[16,256,256]{2,1,0:T(8,128)} %get-tuple-element.10, f32[16,256,256]{2,1,0:T(8,128)} %get-tuple-element.9), kind=kLoop, calls=%fused_computation | loop fusion | flops 2097152 | bytes 16777216 | tf_op jit(solution)/shard_map/concatenate | solution.py:170
  81.7 10.5 %all_to_all.20 = f32[2,4,2,256,512]{4,3,2,1,0:T(8,128)S(1)} all-to-all(f32[2,4,2,256,512]{4,3,2,1,0:T(8,128)S(1)} %bitcast.163), channel_id=1, replica_groups=mesh['z'=4,'y'=4,'x'=4,'core'=2] {'core'}, dimensions={0} | all-to-all | bytes 16777216 | tf_op jit(solution)/shard_map/all_to_all | solution.py:171
  92.2 3.5 fusion.28
  95.7 2.9 copy.46
  98.6 5.9 %fusion.29 = f32[8,256,256]{1,2,0:T(8,128)S(1)} fusion(f32[8,256,256]{2,1,0:T(8,128)} %bitcast.166, f32[8,256,256]{2,1,0:T(8,128)} %bitcast.164), kind=kOutput, calls=%fused_computation.82 | convolution fusion | flops 1610612736 | bytes 6291456 | tf_op jit(solution)/shard_map/hde,hef->hdf/dot_general | solution.py:149
  104.5 0.0 copy-done.6
  104.5 0.0 copy-done.7
  104.5 0.0 copy-done.8
  104.5 3.6 bitcast_add_fusion
  108.2 2.2 pad_maximum_fusion.1
  110.4 5.3 %copy.47 = f32[4,2,256,512]{3,2,1,0:T(8,128)} copy(f32[4,2,256,512]{2,3,1,0:T(8,128)} %bitcast.170) | data formatting | bytes 8388608 | tf_op jit(solution)/shard_map/reshape | solution.py:175
  115.7 53.5 %all_to_all.21 = f32[4,2,256,512]{3,2,1,0:T(8,128)S(1)} all-to-all(f32[4,2,256,512]{3,2,1,0:T(8,128)} %copy.47), channel_id=1, replica_groups=mesh['z'=4,'y'=4,'x'=4,'core'=2] {'x'}, dimensions={0} | all-to-all | bytes 8388608 | tf_op jit(solution)/shard_map/all_to_all | solution.py:176
  169.2 0.7 fusion.22
  169.8 0.7 convolution_add_fusion.14
  170.5 0.7 fusion.21
  171.2 0.7 fusion.20
  171.8 0.7 convolution_add_fusion.13
  172.5 0.7 convolution_add_fusion.12
  173.2 0.1 copy-done.11
  173.3 1.1 pad_maximum_fusion.4
  174.5 0.0 all-gather.5.cloned.1.call-update
  174.5 0.3 all-gather.7.cloned.1.call-start
  174.7 47.6 %all-gather.5.cloned.1.call-done = f32[8,256,512]{2,1,0:T(8,128)} async-done(((f32[2,256,512]{2,1,0:T(8,128)}), f32[8,256,512]{2,1,0:T(8,128)}) %all-gather.5.cloned.1.call-update) | async-done | bytes 4194320 | tf_op jit(solution)/shard_map/all_gather | solution.py:178
  222.3 1.8 fusion.25
  224.2 2.2 convolution_add_fusion.11
  226.4 1.9 fusion.24
  228.3 0.8 copy-done.17
  229.1 1.7 fusion.23
  230.8 1.9 convolution_add_fusion.10
  232.7 0.8 copy-done.19
  233.5 1.8 convolution_add_fusion.9
  235.4 1.1 pad_maximum_fusion.5
  236.5 0.0 all-gather.7.cloned.1.call-update
  236.6 0.6 dynamic-slice
  237.2 46.2 %all-gather.7.cloned.1.call-done = f32[8,256,512]{2,1,0:T(8,128)} async-done(((f32[2,256,512]{2,1,0:T(8,128)}), f32[8,256,512]{2,1,0:T(8,128)}) %all-gather.7.cloned.1.call-update) | async-done | bytes 4194320 | tf_op jit(solution)/shard_map/all_gather | solution.py:180
  283.3 1.8 convolution_add_fusion.8
  285.1 1.9 convolution_add_fusion.7
  287.0 1.9 fusion.7
  288.9 0.8 fusion.13
  289.8 0.7 fusion.4
  290.5 0.7 fusion.5
  291.2 1.9 fusion.6
  293.1 0.2 fusion.10
  293.3 0.7 fusion.2
  294.0 0.2 copy-done.12
  294.1 0.7 fusion.1
  294.8 1.9 fusion.3
  296.7 1.5 pad_maximum_fusion.3
  298.2 4.7 %all-to-all-start.2 = ((f32[4,2,256,256]{3,2,1,0:T(8,128)}), f32[4,2,256,256]{3,2,1,0:T(8,128)}, u32[]{:S(2)}, u32[]{:S(2)}) async-start(f32[4,2,256,256]{3,2,1,0:T(8,128)} %pad_maximum_fusion.3), calls=%async_computation.2 | async-start | bytes 4194304 | tf_op jit(solution)/shard_map/all_to_all | solution.py:190
  302.9 2.9 copy.45
  305.8 23.6 %all-to-all-done.2 = f32[4,2,256,256]{3,2,1,0:T(8,128)} async-done(((f32[4,2,256,256]{3,2,1,0:T(8,128)}), f32[4,2,256,256]{3,2,1,0:T(8,128)}, u32[]{:S(2)}, u32[]{:S(2)}) %all-to-all-start.2) | async-done | bytes 2097184 | tf_op jit(solution)/shard_map/all_to_all | solution.py:190
  329.4 7.7 %fusion = f32[1,8,256,256]{2,3,1,0:T(8,128)} fusion(f32[1,4,2,256,256]{3,4,2,1,0:T(8,128)} %copy.45, f32[8,256,256]{2,1,0:T(8,128)} %bitcast.165, f32[8,256,256]{2,1,0:T(8,128)} %bitcast.45), kind=kOutput, calls=%fused_computation.13 | convolution fusion | flops 1611137024 | bytes 8388608 | tf_op jit(solution)/shard_map/hde,hef->hdf/dot_general | solution.py:149
  337.1 2.9 copy.56
  340.0 2.7 pad_maximum_fusion.2
  342.7 8.2 %all_to_all.22 = f32[2,8,256,256]{2,3,1,0:T(8,128)} all-to-all(f32[2,8,256,256]{2,3,1,0:T(8,128)S(1)} %pad_maximum_fusion.2), channel_id=1, replica_groups=mesh['z'=4,'y'=4,'x'=4,'core'=2] {'core'}, dimensions={0} | all-to-all | bytes 8388608 | tf_op jit(solution)/shard_map/all_to_all | solution.py:192
  350.9 5.5 %copy.59 = f32[2,8,256,256]{3,2,1,0:T(8,128)} copy(f32[2,8,256,256]{2,3,1,0:T(8,128)} %all_to_all.22) | data formatting | bytes 8388608 | tf_op jit(solution)/shard_map/all_to_all | solution.py:192
  356.3 1.6 copy-done.1
  357.9 7.5 %shard_map.65 = bf16[128,4096]{1,0:T(8,128)(2,1)} custom-call(f32[16,256,256]{2,1,0:T(8,128)} %bitcast.169, f32[16,128,256]{2,1,0:T(8,128)S(1)} %get-tuple-element.11.qt_ref, f32[16,128,256]{2,1,0:T(8,128)S(1)} %copy-done.1, bf16[128,4096]{1,0:T(8,128)(2,1)S(1)} %copy-done.3, f32[1,256]{1,0:T(1,128)S(1)} %bitcast.162), custom_call_target="tpu_custom_call" | custom-call | tf_op jit(solution)/shard_map/pallas_call | solution.py:138
  (34 shorter events, 0.1 us)
Async XLA Ops:
  6.5 215.8 %all-gather.5.cloned.1.call-start = ((), (), s32[]{:S(2)}) async-start(), calls=%async_computation.4 | async-start | bytes 5242880 | tf_op jit(solution)/shard_map/all_gather | solution.py:178
  7.4 1.2 copy-start.2
  75.8 1.3 copy-start
  98.6 5.9 %copy-start.6 = (f32[1,4,2,256,256]{4,3,2,1,0:T(8,128)S(1)}, f32[1,4,2,256,256]{4,3,2,1,0:T(8,128)}, u32[]{:S(2)}) copy-start(f32[1,4,2,256,256]{4,3,2,1,0:T(8,128)} %get-tuple-element.13) | copy-start | bytes 6291460
  98.6 5.9 %copy-start.7 = (f32[1,4,2,256,256]{4,3,2,1,0:T(8,128)S(1)}, f32[1,4,2,256,256]{4,3,2,1,0:T(8,128)}, u32[]{:S(2)}) copy-start(f32[1,4,2,256,256]{4,3,2,1,0:T(8,128)} %get-tuple-element.15) | copy-start | bytes 6291460
  98.6 5.9 %copy-start.8 = (f32[1,4,2,256,256]{3,4,2,1,0:T(8,128)S(1)}, f32[1,4,2,256,256]{3,4,2,1,0:T(8,128)}, u32[]{:S(2)}) copy-start(f32[1,4,2,256,256]{3,4,2,1,0:T(8,128)} %copy.46) | copy-start | bytes 6291460
  169.2 3.3 copy-start.5
  170.5 2.0 copy-start.9
  172.5 0.8 copy-start.11
  174.5 108.9 %all-gather.7.cloned.1.call-start = ((), (), s32[]{:S(2)}) async-start(), calls=%async_computation.5 | async-start | bytes 5242880 | tf_op jit(solution)/shard_map/all_gather | solution.py:180
  224.2 6.6 %copy-start.13 = (f32[2,256,256]{2,1,0:T(8,128)}, f32[2,256,256]{2,1,0:T(8,128)S(1)}, u32[]{:S(2)}) copy-start(f32[2,256,256]{2,1,0:T(8,128)S(1)} %fusion.25) | copy-start | bytes 1572868
  226.4 6.3 %copy-start.15 = (f32[2,256,256]{2,1,0:T(8,128)}, f32[2,256,256]{2,1,0:T(8,128)S(1)}, u32[]{:S(2)}) copy-start(f32[2,256,256]{2,1,0:T(8,128)S(1)} %convolution_add_fusion.11) | copy-start | bytes 1572868
  228.3 0.8 copy-start.17
  232.7 0.8 copy-start.19
  287.0 2.8 copy-start.18
  287.0 2.8 copy-start.20
  288.9 1.6 copy-start.14
  288.9 1.6 copy-start.16
  291.2 2.1 copy-start.10
  293.1 1.0 copy-start.12
  298.2 31.3 %all-to-all-start.2 = ((f32[4,2,256,256]{3,2,1,0:T(8,128)}), f32[4,2,256,256]{3,2,1,0:T(8,128)}, u32[]{:S(2)}, u32[]{:S(2)}) async-start(f32[4,2,256,256]{3,2,1,0:T(8,128)} %pad_maximum_fusion.3), calls=%async_computation.2 | async-start | bytes 4194304 | tf_op jit(solution)/shard_map/all_to_all | solution.py:190
  350.9 5.5 %copy-start.3 = (bf16[128,4096]{1,0:T(8,128)(2,1)S(1)}, bf16[128,4096]{1,0:T(8,128)(2,1)}, u32[]{:S(2)}) copy-start(bf16[128,4096]{1,0:T(8,128)(2,1)} %gate_ref.1) | copy-start | bytes 3145732
  350.9 5.5 %copy-start.4 = (f32[256]{0:T(256)S(1)}, f32[256]{0:T(256)}, u32[]{:S(2)}) copy-start(f32[256]{0:T(256)} %param.11) | copy-start | bytes 3076
  356.3 1.6 copy-start.1
Sparse Core Ops, SparseCore 0:
  174.6 47.7 all-gather.4
  236.7 46.6 all-gather.6

commit v2 on v1

v2 whole, which is shorter than its diff:
```python
import functools

import jax
import jax.numpy as jnp
from jax import lax
from jax.experimental import pallas as pl
from jax.experimental.pallas import tpu as pltpu
from jax.sharding import Mesh
from jax.sharding import PartitionSpec as P

H = 16
DK = 256
CT = 128
STEPS = 256
EPS = 1e-06
LEVELS = 8
f32 = jnp.float32
bf16 = jnp.bfloat16
AXES = ("z", "y", "x", "core")
MESH = pl.DeviceIdType.MESH


def mm(a, b, dims=((1,), (0,))):
    return lax.dot_general(a, b, (dims, ((), ())), preferred_element_type=f32)


def split(x):
    hi = x.astype(bf16)
    return hi, (x - hi.astype(f32)).astype(bf16)


def mm_right(a, b):
    hi, lo = b
    return mm(a, hi) + mm(a, lo)


def mm_both(a, b):
    return mm(a[0], b[0]) + (mm(a[0], b[1]) + mm(a[1], b[0]))


def factors(ks, vs, qs, beta_rows, mask_ref):
    row = lax.broadcasted_iota(jnp.int32, (STEPS, STEPS), 0)
    col = lax.broadcasted_iota(jnp.int32, (STEPS, STEPS), 1)
    eye = row == col
    n = range(len(ks))
    gram = [mm(k, k, ((1,), (1,))) for k in ks]
    g = [jnp.sum(jnp.where(eye, x, 0.0), axis=0, keepdims=True) + EPS for x in gram]
    c = [beta_rows[i] / g[i] for i in n]
    low = [split(jnp.where(row > col, x, 0.0)) for x in gram]
    tau = [jnp.where(eye, x, 0.0) for x in c]
    for level in range(LEVELS):
        edge = [x[0] * mask_ref[level] for x in low]
        tb = [x.astype(bf16) for x in tau]
        if level == 0:
            step = [(edge[i].astype(f32) * c[i]).astype(bf16) for i in n]
        else:
            step = [mm(edge[i], tb[i]).astype(bf16) for i in n]
        tau = [tau[i] - mm(tb[i], step[i]) for i in n]
    tb = [x.astype(bf16) for x in tau]
    t32 = [x.astype(f32) for x in tb]
    rest = [
        jnp.where(eye, 1.0, 0.0) - t32[i] * (g[i] / beta_rows[i]) - mm_right(tb[i], low[i]) for i in n
    ]
    tau = [t32[i] + mm(rest[i].astype(bf16), tb[i]) for i in n]
    ts = [split(x) for x in tau]
    w = [split(mm(ts[i][0], ks[i]) + mm(ts[i][1], ks[i])) for i in n]
    ts = [split(tau[i] * jnp.sqrt(g[i])) for i in n]
    y = [split(mm(ts[i][0], vs[i]) + mm(ts[i][1], vs[i])) for i in n]
    kt = [k.T for k in ks]
    a = [jnp.where(eye, 1.0, 0.0) - mm_right(kt[i], w[i]) for i in n]
    b = [mm_right(kt[i], y[i]) for i in n]
    token = lax.broadcasted_iota(jnp.int32, (CT, STEPS), 0)
    step_of = lax.broadcasted_iota(jnp.int32, (CT, STEPS), 1)
    causal = step_of // 2 <= token
    p = [split(jnp.where(causal, mm(qs[i], ks[i], ((1,), (1,))), 0.0)) for i in n]
    q32 = [q.astype(f32) for q in qs]
    unit = [lax.rsqrt(jnp.sum(q * q, axis=-1, keepdims=True) + EPS) for q in q32]
    qt = [(q32[i] - mm_both(p[i], w[i])) * unit[i] for i in n]
    ot = [mm_both(p[i], y[i]) * unit[i] for i in n]
    return a, b, qt, ot


def make_masks(mask_ref):
    row = lax.broadcasted_iota(jnp.int32, (STEPS, STEPS), 0)
    col = lax.broadcasted_iota(jnp.int32, (STEPS, STEPS), 1)
    differ = jnp.bitwise_xor(row, col)
    for level in range(LEVELS):
        inside = (differ >= (1 << level)) & (differ < (2 << level))
        mask_ref[level] = jnp.where(inside, 1.0, 0.0).astype(bf16)


def gated(o, gain, gate):
    scale = lax.rsqrt(jnp.mean(o * o, axis=-1, keepdims=True) + EPS)
    normed = (o * scale * gain).astype(bf16).astype(f32)
    gate = gate.astype(f32)
    return (normed * (gate / (1.0 + jnp.exp(-gate)))).astype(bf16)


def put_pair(ref, values):
    ref[0], ref[1] = split(values)


def layer_kernel(
    q_ref, k_ref, v_ref, beta_ref, gate_ref, gain_ref, out_ref,
    mask, qt, ot, blk, x_out, x_in, pxa, pxb, y_in, pya, pyb, line_a, line_b, z_in, z_out,
    s_out, s_in, mine, c_out, c_in,
    core_send, core_recv, x_send, x_recv, y_send, y_recv, z_send, z_recv, s_send, s_recv,
    c_send, c_recv, here,
):
    z, y, x, c = (lax.axis_index(name) for name in AXES)
    other = {"core": 1 - c}

    def along(axis, index, offset):
        return {axis: lax.rem(index + offset, 4)}

    barrier = pltpu.get_barrier_semaphore()
    greeted = [other] + [along("x", x, o) for o in (1, 2, 3)] + [along("y", y, o) for o in (1, 2, 3)]
    greeted += [along("z", z, o) for o in (1, 3)]
    for device in greeted:
        pl.semaphore_signal(barrier, inc=1, device_id=device, device_id_type=MESH)

    def remote(src, dst, send, recv, device):
        return pltpu.make_async_remote_copy(
            src_ref=src, dst_ref=dst, send_sem=send, recv_sem=recv, device_id=device, device_id_type=MESH
        )

    def core_copy(j, slot):
        return remote(blk.at[2, j], blk.at[slot, j], core_send.at[j], core_recv.at[j], other)

    def x_copy(i, o, j, source):
        return remote(
            x_out.at[j], x_in.at[source, i], x_send.at[o, i], x_recv.at[source, i], along("x", x, o)
        )

    def y_copy(i, o, source):
        return remote(
            y_in.at[y, i], y_in.at[source, i], y_send.at[o, i], y_recv.at[source, i], along("y", y, o)
        )

    def z_copy(i):
        return remote(z_out.at[i], z_in.at[i], z_send.at[i], z_recv.at[i], along("z", z, 1))

    def s_copy(i, o, dest, source):
        j = 2 * source + i
        return remote(s_out.at[dest, i], s_in.at[j], s_send.at[o, i], s_recv.at[j], along("x", x, o))

    def c_copy(j):
        return remote(c_out.at[j], c_in.at[j], c_send.at[j], c_recv.at[j], other)

    def lanes_of(head):
        return pl.ds(pl.multiple_of(head * DK, DK), DK)

    make_masks(mask)

    def phase(p, carry):
        i, own = p // 2, p % 2
        group = own * c + (1 - own) * (1 - c)
        slot = own * c + (1 - own) * 2
        heads = [8 * group + 2 * n + i for n in range(4)]
        lanes = [lanes_of(h) for h in heads]
        a, b, q_now, o_now = factors(
            [k_ref[:, :, n].reshape(STEPS, DK) for n in lanes],
            [v_ref[:, :, n].reshape(STEPS, DK) for n in lanes],
            [q_ref[:, n] for n in lanes],
            [beta_ref[h] for h in heads],
            mask,
        )
        for n in range(4):
            j = 2 * n + i
            put_pair(blk.at[slot, j, pl.ds(0, 2)], a[n])
            put_pair(blk.at[slot, j, pl.ds(2, 2)], b[n])
            qt[heads[n]] = q_now[n]
            ot[heads[n]] = o_now[n]

        @pl.when(p == 0)
        def _():
            pl.semaphore_wait(barrier, len(greeted))

        @pl.when(own == 0)
        def _():
            for n in range(4):
                core_copy(2 * n + i, c).start()

        @pl.when(own == 1)
        def _():
            for o in (1, 3, 2, 0):
                dest = lax.rem(x + o, 4)
                j = 2 * dest + i
                core_copy(j, 1 - c).wait_recv()
                later = (blk[1, j, 0], blk[1, j, 1])
                put_pair(x_out.at[j, pl.ds(0, 2)], mm_both(later, (blk[0, j, 0], blk[0, j, 1])))
                x_out[j, 2] = (
                    mm_both(later, (blk[0, j, 2], blk[0, j, 3]))
                    + blk[1, j, 2].astype(f32)
                    + blk[1, j, 3].astype(f32)
                ).astype(bf16)
                if o:
                    x_copy(i, o, j, x).start()
                else:
                    pltpu.make_async_copy(x_out.at[j], x_in.at[x, i], here.at[i]).start()

        return carry

    lax.fori_loop(0, 4, phase, 0)

    def compose(pairs, i, pa, pb):
        eye = lax.broadcasted_iota(jnp.int32, (DK, DK), 0) == lax.broadcasted_iota(jnp.int32, (DK, DK), 1)
        pa[i, 0, 0] = jnp.where(eye, 1.0, 0.0).astype(bf16)
        pa[i, 0, 1] = jnp.zeros((DK, DK), bf16)
        pb[i, 0] = jnp.zeros((DK, DK), f32)
        a = (pairs[0, i, 0], pairs[0, i, 1])
        b = pairs[0, i, 2].astype(f32)
        for n in range(1, 4):
            pa[i, n, 0], pa[i, n, 1] = a
            pb[i, n] = b
            later = (pairs[n, i, 0], pairs[n, i, 1])
            a = split(mm_both(later, a))
            b = mm_both(later, split(b)) + pairs[n, i, 2].astype(f32)
        return a, b

    def over_x(i, carry):
        pltpu.make_async_copy(x_out.at[2 * x + i], x_in.at[x, i], here.at[i]).wait()
        for o in (1, 3, 2):
            source = lax.rem(x + o, 4)
            x_copy(i, o, 2 * source + i, source).wait_recv()
        a, b = compose(x_in, i, pxa, pxb)
        y_in[y, i, 0], y_in[y, i, 1] = a
        y_in[y, i, 2] = b.astype(bf16)
        for o in (1, 3, 2):
            y_copy(i, o, y).start()
        return carry

    lax.fori_loop(0, 2, over_x, 0)

    def over_y(i, carry):
        for o in (1, 3, 2):
            y_copy(i, o, lax.rem(y + o, 4)).wait_recv()
        a, b = compose(y_in, i, pya, pyb)
        line_a[i, 0], line_a[i, 1] = a
        line_b[i] = b

        @pl.when(z == 0)
        def _():
            z_in[i] = jnp.zeros((DK, DK), bf16)

        @pl.when(z > 0)
        def _():
            z_copy(i).wait_recv()

        @pl.when(z < 3)
        def _():
            s = z_in[i]
            z_out[i] = (mm(line_a[i, 0], s) + mm(line_a[i, 1], s) + line_b[i]).astype(bf16)
            z_copy(i).start()

        s = z_in[i]
        s = split(mm(pya[i, y, 0], s) + mm(pya[i, y, 1], s) + pyb[i, y])
        for o in (1, 3, 2, 0):
            dest = lax.rem(x + o, 4)
            now = (mm_both((pxa[i, dest, 0], pxa[i, dest, 1]), s) + pxb[i, dest]).astype(bf16)
            if o:
                s_out[dest, i] = now
                s_copy(i, o, dest, x).start()
            else:
                s_in[2 * x + i] = now
        return carry

    lax.fori_loop(0, 2, over_y, 0)

    def over_cores(i, carry):
        for o in (0, 1, 3, 2):
            source = lax.rem(x + o, 4)
            j = 2 * source + i
            if o:
                s_copy(i, o, source, source).wait_recv()
            first = s_in[j]
            second = (
                mm(blk[0, j, 0], first)
                + mm(blk[0, j, 1], first)
                + blk[0, j, 2].astype(f32)
                + blk[0, j, 3].astype(f32)
            ).astype(bf16)
            mine[j] = jnp.where(c == 0, first, second)
            c_out[j] = jnp.where(c == 0, second, first)
            c_copy(j).start()
        return carry

    lax.fori_loop(0, 2, over_cores, 0)

    def finish(head, state):
        q_now = split(qt[head])
        o = mm(q_now[0], state) + mm(q_now[1], state) + ot[head]
        lanes = lanes_of(head)
        out_ref[:, lanes] = gated(o, gain_ref[...], gate_ref[:, lanes])

    def last_own(j, carry):
        finish(8 * c + j, mine[j])
        return carry

    def last_other(j, carry):
        c_copy(j).wait_recv()
        finish(8 * (1 - c) + j, c_in[j])
        return carry

    lax.fori_loop(0, 8, last_own, 0)
    lax.fori_loop(0, 8, last_other, 0)

    def drain(j, carry):
        core_copy(j, c).wait_send()
        c_copy(j).wait_send()
        return carry

    def drain_links(i, carry):
        for o in (1, 2, 3):
            dest = lax.rem(x + o, 4)
            x_copy(i, o, 2 * dest + i, x).wait_send()
            y_copy(i, o, y).wait_send()
            s_copy(i, o, dest, x).wait_send()

        @pl.when(z < 3)
        def _():
            z_copy(i).wait_send()

        return carry

    lax.fori_loop(0, 8, drain, 0)
    lax.fori_loop(0, 2, drain_links, 0)


def shards(queries, keys, values, betas, gate, norm_gain):
    beta_rows = betas.astype(f32).transpose(2, 0, 1).reshape(H, 1, STEPS)
    here = pl.BlockSpec(memory_space=pltpu.VMEM)
    vm = pltpu.VMEM
    dma = pltpu.SemaphoreType.DMA
    tile = (DK, DK)
    return pl.pallas_call(
        layer_kernel,
        in_specs=[here] * 6,
        out_specs=here,
        out_shape=jax.ShapeDtypeStruct((CT, H * DK), bf16),
        scratch_shapes=[
            vm((LEVELS, STEPS, STEPS), bf16),
            vm((H, CT, DK), f32),
            vm((H, CT, DK), f32),
            vm((3, 8, 4) + tile, bf16),
            vm((8, 3) + tile, bf16),
            vm((4, 2, 3) + tile, bf16),
            vm((2, 4, 2) + tile, bf16),
            vm((2, 4) + tile, f32),
            vm((4, 2, 3) + tile, bf16),
            vm((2, 4, 2) + tile, bf16),
            vm((2, 4) + tile, f32),
            vm((2, 2) + tile, bf16),
            vm((2,) + tile, f32),
            vm((2,) + tile, bf16),
            vm((2,) + tile, bf16),
            vm((4, 2) + tile, bf16),
            vm((8,) + tile, bf16),
            vm((8,) + tile, bf16),
            vm((8,) + tile, bf16),
            vm((8,) + tile, bf16),
            dma((8,)),
            dma((8,)),
            dma((4, 2)),
            dma((4, 2)),
            dma((4, 2)),
            dma((4, 2)),
            dma((2,)),
            dma((2,)),
            dma((4, 2)),
            dma((8,)),
            dma((8,)),
            dma((8,)),
            dma((2,)),
        ],
        compiler_params=pltpu.CompilerParams(
            collective_id=0, has_side_effects=True, vmem_limit_bytes=60 << 20
        ),
    )(queries, keys, values, beta_rows, gate, norm_gain.reshape(1, DK))


def solution(mesh):
    torus = Mesh(mesh.devices.reshape(4, 4, 4, 2), AXES)
    rows, pairs = P(AXES, None), P(AXES, None, None)
    return jax.shard_map(
        shards, mesh=torus, in_specs=(rows, pairs, pairs, pairs, rows, P()), out_specs=rows, check_vma=False
    )
```

time: 378 us -> 103 us (0.27); the launches traced: 372 us -> 103 us
  waiting for transfers between devices: 117 us -> 0 us
  blocking collectives: 72.1 us -> 0 us
  matrix products: 44.3 us -> 0 us
  local copies, waits for them, and re-layouts: 29.9 us -> 3.08 us
  Pallas kernels: 74.6 us -> 99.1 us
  other arithmetic: 14.9 us -> 0.7 us
  between operations: 13.8 us -> 0.01 us
  starting transfers between devices: 5 us -> 0 us
    all_gather x2 -> x0, waiting for transfers between devices: 93.8 us -> none  [the longest x1 47.6 us: shards(): ab = lax.all_gather(jnp.concatenate(in_x[-1], axis=-1), 'y')]
    all_to_all x3 -> x0, blocking collectives: 72.1 us -> none  [the longest x1 53.5 us: shards(): ab = lax.all_to_all(ab, 'x', 0, 0, tiled=True)]
    dot_general x24 -> x0, matrix products: 44.3 us -> none  [einmul(): return jnp.einsum('hde,hef->hdf', a, b, precision=highest)]
    pallas_call x2 -> x1, Pallas kernels: 74.6 us -> 99.1 us  [shards(): pl.pallas_call(layer_kernel, in_specs=[here] * 6, out_specs=here, out_sha...]
    all_to_all x1 -> x0, waiting for transfers between devices: 23.6 us -> none  [shards(): states = lax.all_to_all(states, 'x', 0, 0, tiled=True).reshape(8, DK, DK)]
    slice x3 -> x0, local copies, waits for them, and re-layouts: 9.33 us -> none  [the longest x2 5.8 us: shards(): ab[i, ..., DK:].reshape(8, DK, DK)]
    concatenate x4 -> x0, other arithmetic: 9 us -> none  [the longest x1 4.52 us: shards(): ab = jnp.concatenate([a, b], axis=-1).reshape(2, 4, 2, DK, 2 * DK)]
    all_to_all x2 -> x0, local copies, waits for them, and re-layouts: 8.33 us -> none  [the longest x1 5.45 us: shards(): lax.all_to_all(jnp.stack([states, later]), 'core', 0, 0, tiled=True)]
  transfers between devices with their start and end apart: 3 -> 0, of which waited for: 3 -> 0; matrix products, arithmetic and copies ran while one was open for 1% -> 0% of each run, Pallas kernels for 0% -> 0%
where the time goes in v2:
time: 103 us
  Pallas kernels  99.1 us (96%)
  local copies, waits for them, and re-layouts  3.08 us (3%)
    pallas_call x1, Pallas kernels, shards(): pl.pallas_call(layer_kernel, in_specs=[here] * 6, out_specs=here, out_sha...  99.1 us
    unnamed x1, local copies, waits for them, and re-layouts  2.29 us

profile of v2, /device:TPU:96, one launch (start us, length us, event | category | flops | bytes accessed | tf_op | source)
XLA Modules:
  0.0 102.9 jit_solution(12174531686429457426)
XLA Ops:
  0.0 0.7 convert_bitcast_fusion
  0.7 0.1 copy.8
  0.8 0.7 copy.9.beta_ref
  1.5 99.1 %shard_map.64 = bf16[128,4096]{1,0:T(8,128)(2,1)} custom-call(bf16[128,4096]{1,0:T(8,128)(2,1)} %q_ref.1, bf16[128,2,4096]{2,1,0:T(2,128)(2,1)} %k_ref.1, bf16[128,2,4096]{2,1,0:T(2,128)(2,1)} %v_ref.1, f32[16,1,256]{2,1,0:T(1,128)} %copy.9.beta_ref, bf16[128,4096]{1,0:T(8,128)(2,1)} %gate_ref.1, f32[1,256]{1,0:T(1,128)} %bitcast.5), custom_call_target="tpu_custom_call" | custom-call | tf_op jit(solution)/shard_map/pallas_call | solution.py:336
  100.6 2.3 %copy.11 = bf16[128,4096]{1,0:T(8,128)(2,1)} copy(bf16[128,4096]{1,0:T(8,128)(2,1)} %shard_map.64) | data formatting | bytes 2097152

commit v3 on v2

--- a/solution.py
+++ b/solution.py
@@ -14,6 +14,7 @@
 STEPS = 256
 EPS = 1e-06
 LEVELS = 8
+HALF = 128
 f32 = jnp.float32
 bf16 = jnp.bfloat16
 AXES = ("z", "y", "x", "core")
@@ -38,25 +39,44 @@
     return mm(a[0], b[0]) + (mm(a[0], b[1]) + mm(a[1], b[0]))
 
 
-def factors(ks, vs, qs, beta_rows, mask_ref):
+def factors(ks, vs, beta_rows, mask_ref):
     row = lax.broadcasted_iota(jnp.int32, (STEPS, STEPS), 0)
     col = lax.broadcasted_iota(jnp.int32, (STEPS, STEPS), 1)
     eye = row == col
+    eye_h = eye[:HALF, :HALF]
     n = range(len(ks))
+    both = range(2)
+    part = (slice(0, HALF), slice(HALF, STEPS))
     gram = [mm(k, k, ((1,), (1,))) for k in ks]
     g = [jnp.sum(jnp.where(eye, x, 0.0), axis=0, keepdims=True) + EPS for x in gram]
     c = [beta_rows[i] / g[i] for i in n]
     low = [split(jnp.where(row > col, x, 0.0)) for x in gram]
-    tau = [jnp.where(eye, x, 0.0) for x in c]
-    for level in range(LEVELS):
-        edge = [x[0] * mask_ref[level] for x in low]
-        tb = [x.astype(bf16) for x in tau]
+    tau = [[jnp.where(eye_h, c[i][:, part[j]], 0.0) for j in both] for i in n]
+    diag = [[low[i][0][part[j], part[j]] for j in both] for i in n]
+    for level in range(LEVELS - 1):
+        edge = [[x * mask_ref[level] for x in d] for d in diag]
+        tb = [[x.astype(bf16) for x in t] for t in tau]
         if level == 0:
-            step = [(edge[i].astype(f32) * c[i]).astype(bf16) for i in n]
+            step = [
+                [(edge[i][j].astype(f32) * c[i][:, part[j]]).astype(bf16) for j in both] for i in n
+            ]
         else:
-            step = [mm(edge[i], tb[i]).astype(bf16) for i in n]
-        tau = [tau[i] - mm(tb[i], step[i]) for i in n]
-    tb = [x.astype(bf16) for x in tau]
+            step = [[mm(edge[i][j], tb[i][j]).astype(bf16) for j in both] for i in n]
+        tau = [[tau[i][j] - mm(tb[i][j], step[i][j]) for j in both] for i in n]
+    tb = [[x.astype(bf16) for x in t] for t in tau]
+    step = [mm(low[i][0][part[1], part[0]], tb[i][0]).astype(bf16) for i in n]
+    below = [-mm(tb[i][1], step[i]) for i in n]
+    zero = jnp.zeros((HALF, HALF), bf16)
+    tb = [
+        jnp.concatenate(
+            [
+                jnp.concatenate([tb[i][0], zero], axis=1),
+                jnp.concatenate([below[i].astype(bf16), tb[i][1]], axis=1),
+            ],
+            axis=0,
+        )
+        for i in n
+    ]
     t32 = [x.astype(f32) for x in tb]
     rest = [
         jnp.where(eye, 1.0, 0.0) - t32[i] * (g[i] / beta_rows[i]) - mm_right(tb[i], low[i]) for i in n
@@ -69,6 +89,11 @@
     kt = [k.T for k in ks]
     a = [jnp.where(eye, 1.0, 0.0) - mm_right(kt[i], w[i]) for i in n]
     b = [mm_right(kt[i], y[i]) for i in n]
+    return a, b, w, y
+
+
+def answers(ks, qs, w, y):
+    n = range(len(ks))
     token = lax.broadcasted_iota(jnp.int32, (CT, STEPS), 0)
     step_of = lax.broadcasted_iota(jnp.int32, (CT, STEPS), 1)
     causal = step_of // 2 <= token
@@ -77,14 +102,14 @@
     unit = [lax.rsqrt(jnp.sum(q * q, axis=-1, keepdims=True) + EPS) for q in q32]
     qt = [(q32[i] - mm_both(p[i], w[i])) * unit[i] for i in n]
     ot = [mm_both(p[i], y[i]) * unit[i] for i in n]
-    return a, b, qt, ot
+    return qt, ot
 
 
 def make_masks(mask_ref):
-    row = lax.broadcasted_iota(jnp.int32, (STEPS, STEPS), 0)
-    col = lax.broadcasted_iota(jnp.int32, (STEPS, STEPS), 1)
+    row = lax.broadcasted_iota(jnp.int32, (HALF, HALF), 0)
+    col = lax.broadcasted_iota(jnp.int32, (HALF, HALF), 1)
     differ = jnp.bitwise_xor(row, col)
-    for level in range(LEVELS):
+    for level in range(LEVELS - 1):
         inside = (differ >= (1 << level)) & (differ < (2 << level))
         mask_ref[level] = jnp.where(inside, 1.0, 0.0).astype(bf16)
 
@@ -102,9 +127,9 @@
 
 def layer_kernel(
     q_ref, k_ref, v_ref, beta_ref, gate_ref, gain_ref, out_ref,
-    mask, qt, ot, blk, x_out, x_in, pxa, pxb, y_in, pya, pyb, line_a, line_b, z_in, z_out,
+    mask, wy, blk, x_out, x_in, pxa, pxb, y_out, y_in, pya, pyb, z_in, z_out, u_out, u_in,
     s_out, s_in, mine, c_out, c_in,
-    core_send, core_recv, x_send, x_recv, y_send, y_recv, z_send, z_recv, s_send, s_recv,
+    core_send, core_recv, x_send, x_recv, y_send, y_recv, z_send, z_recv, u_send, u_recv, s_send, s_recv,
     c_send, c_recv, here,
 ):
     z, y, x, c = (lax.axis_index(name) for name in AXES)
@@ -132,13 +157,14 @@
             x_out.at[j], x_in.at[source, i], x_send.at[o, i], x_recv.at[source, i], along("x", x, o)
         )
 
-    def y_copy(i, o, source):
-        return remote(
-            y_in.at[y, i], y_in.at[source, i], y_send.at[o, i], y_recv.at[source, i], along("y", y, o)
-        )
-
-    def z_copy(i):
-        return remote(z_out.at[i], z_in.at[i], z_send.at[i], z_recv.at[i], along("z", z, 1))
+    def y_copy(i, source, root):
+        return remote(y_out.at[i], y_in.at[source], y_send.at[i], y_recv.at[source], {"y": root})
+
+    def z_copy():
+        return remote(z_out, z_in, z_send.at[0], z_recv.at[0], along("z", z, 1))
+
+    def u_copy(i, o, dest):
+        return remote(u_out.at[dest], u_in.at[i], u_send.at[o], u_recv.at[i], {"y": dest})
 
     def s_copy(i, o, dest, source):
         j = 2 * source + i
@@ -158,10 +184,9 @@
         slot = own * c + (1 - own) * 2
         heads = [8 * group + 2 * n + i for n in range(4)]
         lanes = [lanes_of(h) for h in heads]
-        a, b, q_now, o_now = factors(
+        a, b, w, y = factors(
             [k_ref[:, :, n].reshape(STEPS, DK) for n in lanes],
             [v_ref[:, :, n].reshape(STEPS, DK) for n in lanes],
-            [q_ref[:, n] for n in lanes],
             [beta_ref[h] for h in heads],
             mask,
         )
@@ -169,8 +194,8 @@
             j = 2 * n + i
             put_pair(blk.at[slot, j, pl.ds(0, 2)], a[n])
             put_pair(blk.at[slot, j, pl.ds(2, 2)], b[n])
-            qt[heads[n]] = q_now[n]
-            ot[heads[n]] = o_now[n]
+            wy[heads[n], 0], wy[heads[n], 1] = w[n]
+            wy[heads[n], 2], wy[heads[n], 3] = y[n]
 
         @pl.when(p == 0)
         def _():
@@ -203,58 +228,99 @@
 
     lax.fori_loop(0, 4, phase, 0)
 
-    def compose(pairs, i, pa, pb):
+    def answer(p, carry):
+        heads = [4 * p + n for n in range(4)]
+        lanes = [lanes_of(h) for h in heads]
+        q_now, o_now = answers(
+            [k_ref[:, :, n].reshape(STEPS, DK) for n in lanes],
+            [q_ref[:, n] for n in lanes],
+            [(wy[h, 0], wy[h, 1]) for h in heads],
+            [(wy[h, 2], wy[h, 3]) for h in heads],
+        )
+        for n in range(4):
+            h = heads[n]
+            wy[h, 0, :CT], wy[h, 0, CT:] = split(q_now[n])
+            wy[h, 1, :CT], wy[h, 1, CT:] = split(o_now[n])
+        return carry
+
+    lax.fori_loop(0, 4, answer, 0)
+
+    def compose(pairs, pa, pb):
         eye = lax.broadcasted_iota(jnp.int32, (DK, DK), 0) == lax.broadcasted_iota(jnp.int32, (DK, DK), 1)
-        pa[i, 0, 0] = jnp.where(eye, 1.0, 0.0).astype(bf16)
-        pa[i, 0, 1] = jnp.zeros((DK, DK), bf16)
-        pb[i, 0] = jnp.zeros((DK, DK), f32)
-        a = (pairs[0, i, 0], pairs[0, i, 1])
-        b = pairs[0, i, 2].astype(f32)
+        pa[0, 0] = jnp.where(eye, 1.0, 0.0).astype(bf16)
+        pa[0, 1] = jnp.zeros((DK, DK), bf16)
+        pb[0] = jnp.zeros((DK, DK), f32)
+        a = (pairs[0, 0], pairs[0, 1])
+        b = pairs[0, 2].astype(f32)
         for n in range(1, 4):
-            pa[i, n, 0], pa[i, n, 1] = a
-            pb[i, n] = b
-            later = (pairs[n, i, 0], pairs[n, i, 1])
+            pa[n, 0], pa[n, 1] = a
+            pb[n] = b
+            later = (pairs[n, 0], pairs[n, 1])
             a = split(mm_both(later, a))
-            b = mm_both(later, split(b)) + pairs[n, i, 2].astype(f32)
+            b = mm_both(later, split(b)) + pairs[n, 2].astype(f32)
         return a, b
 
-    def over_x(i, carry):
+    def over_x(i):
         pltpu.make_async_copy(x_out.at[2 * x + i], x_in.at[x, i], here.at[i]).wait()
         for o in (1, 3, 2):
             source = lax.rem(x + o, 4)
             x_copy(i, o, 2 * source + i, source).wait_recv()
-        a, b = compose(x_in, i, pxa, pxb)
-        y_in[y, i, 0], y_in[y, i, 1] = a
-        y_in[y, i, 2] = b.astype(bf16)
+        a, b = compose(x_in.at[:, i], pxa.at[i], pxb.at[i])
+        root = 2 * c + i
+
+        @pl.when(y == root)
+        def _():
+            y_in[y, 0], y_in[y, 1] = a
+            y_in[y, 2] = b.astype(bf16)
+
+        @pl.when(y != root)
+        def _():
+            y_out[i, 0], y_out[i, 1] = a
+            y_out[i, 2] = b.astype(bf16)
+            y_copy(i, y, root).start()
+
+    i_root = y % 2
+    is_root = y // 2 == c
+
+    def over_y():
         for o in (1, 3, 2):
-            y_copy(i, o, y).start()
-        return carry
-
-    lax.fori_loop(0, 2, over_x, 0)
-
-    def over_y(i, carry):
-        for o in (1, 3, 2):
-            y_copy(i, o, lax.rem(y + o, 4)).wait_recv()
-        a, b = compose(y_in, i, pya, pyb)
-        line_a[i, 0], line_a[i, 1] = a
-        line_b[i] = b
-
+            y_copy(i_root, lax.rem(y + o, 4), y).wait_recv()
+        a, b = compose(y_in, pya, pyb)
+        z_out[...] = b.astype(bf16)
+        pya[4, 0], pya[4, 1] = a
+        pyb[4] = b
+
+    def over_z():
         @pl.when(z == 0)
         def _():
-            z_in[i] = jnp.zeros((DK, DK), bf16)
+            z_in[...] = jnp.zeros((DK, DK), bf16)
 
         @pl.when(z > 0)
         def _():
-            z_copy(i).wait_recv()
+            z_copy().wait_recv()
+            z_out[...] = (mm(pya[4, 0], z_in[...]) + mm(pya[4, 1], z_in[...]) + pyb[4]).astype(bf16)
 
         @pl.when(z < 3)
         def _():
-            s = z_in[i]
-            z_out[i] = (mm(line_a[i, 0], s) + mm(line_a[i, 1], s) + line_b[i]).astype(bf16)
-            z_copy(i).start()
-
-        s = z_in[i]
-        s = split(mm(pya[i, y, 0], s) + mm(pya[i, y, 1], s) + pyb[i, y])
+            z_copy().start()
+
+        for o in (1, 3, 2, 0):
+            dest = lax.rem(y + o, 4)
+            now = mm(pya[dest, 0], z_in[...]) + mm(pya[dest, 1], z_in[...]) + pyb[dest]
+            if o:
+                put_pair(u_out.at[dest], now)
+                u_copy(i_root, o, dest).start()
+            else:
+                put_pair(u_in.at[i_root], now)
+
+    def down(i):
+        root = 2 * c + i
+
+        @pl.when(y != root)
+        def _():
+            u_copy(i, 1, y).wait_recv()
+
+        s = (u_in[i, 0], u_in[i, 1])
         for o in (1, 3, 2, 0):
             dest = lax.rem(x + o, 4)
             now = (mm_both((pxa[i, dest, 0], pxa[i, dest, 1]), s) + pxb[i, dest]).astype(bf16)
@@ -263,9 +329,18 @@
                 s_copy(i, o, dest, x).start()
             else:
                 s_in[2 * x + i] = now
-        return carry
-
-    lax.fori_loop(0, 2, over_y, 0)
+
+    first_root = is_root & (i_root == 0)
+    second_root = is_root & (i_root == 1)
+    over_x(0)
+    pl.when(first_root)(over_y)
+    over_x(1)
+    pl.when(first_root)(over_z)
+    pl.when(second_root)(over_y)
+    pl.when(second_root & (z < 2))(over_z)
+    down(0)
+    pl.when(second_root & (z >= 2))(over_z)
+    down(1)
 
     def over_cores(i, carry):
         for o in (0, 1, 3, 2):
@@ -288,8 +363,8 @@
     lax.fori_loop(0, 2, over_cores, 0)
 
     def finish(head, state):
-        q_now = split(qt[head])
-        o = mm(q_now[0], state) + mm(q_now[1], state) + ot[head]
+        o = mm(wy[head, 0, :CT], state) + mm(wy[head, 0, CT:], state)
+        o += wy[head, 1, :CT].astype(f32) + wy[head, 1, CT:].astype(f32)
         lanes = lanes_of(head)
         out_ref[:, lanes] = gated(o, gain_ref[...], gate_ref[:, lanes])
 
@@ -314,17 +389,25 @@
         for o in (1, 2, 3):
             dest = lax.rem(x + o, 4)
             x_copy(i, o, 2 * dest + i, x).wait_send()
-            y_copy(i, o, y).wait_send()
             s_copy(i, o, dest, x).wait_send()
 
-        @pl.when(z < 3)
-        def _():
-            z_copy(i).wait_send()
+        @pl.when(y != 2 * c + i)
+        def _():
+            y_copy(i, y, 2 * c + i).wait_send()
 
         return carry
 
     lax.fori_loop(0, 8, drain, 0)
     lax.fori_loop(0, 2, drain_links, 0)
+
+    @pl.when(is_root)
+    def _():
+        for o in (1, 2, 3):
+            u_copy(i_root, o, lax.rem(y + o, 4)).wait_send()
+
+        @pl.when(z < 3)
+        def _():
+            z_copy().wait_send()
 
 
 def shards(queries, keys, values, betas, gate, norm_gain):
@@ -339,21 +422,21 @@
         out_specs=here,
         out_shape=jax.ShapeDtypeStruct((CT, H * DK), bf16),
         scratch_shapes=[
-            vm((LEVELS, STEPS, STEPS), bf16),
-            vm((H, CT, DK), f32),
-            vm((H, CT, DK), f32),
+            vm((LEVELS - 1, HALF, HALF), bf16),
+            vm((H, 4) + tile, bf16),
             vm((3, 8, 4) + tile, bf16),
             vm((8, 3) + tile, bf16),
             vm((4, 2, 3) + tile, bf16),
             vm((2, 4, 2) + tile, bf16),
             vm((2, 4) + tile, f32),
-            vm((4, 2, 3) + tile, bf16),
-            vm((2, 4, 2) + tile, bf16),
-            vm((2, 4) + tile, f32),
+            vm((2, 3) + tile, bf16),
+            vm((4, 3) + tile, bf16),
+            vm((5, 2) + tile, bf16),
+            vm((5,) + tile, f32),
+            vm(tile, bf16),
+            vm(tile, bf16),
+            vm((4, 2) + tile, bf16),
             vm((2, 2) + tile, bf16),
-            vm((2,) + tile, f32),
-            vm((2,) + tile, bf16),
-            vm((2,) + tile, bf16),
             vm((4, 2) + tile, bf16),
             vm((8,) + tile, bf16),
             vm((8,) + tile, bf16),
@@ -363,9 +446,11 @@
             dma((8,)),
             dma((4, 2)),
             dma((4, 2)),
-            dma((4, 2)),
-            dma((4, 2)),
             dma((2,)),
+            dma((4,)),
+            dma((1,)),
+            dma((1,)),
+            dma((4,)),
             dma((2,)),
             dma((4, 2)),
             dma((8,)),

time: 103 us -> 102 us (level)
  the two profiles are of different devices: /device:TPU:96 before, /device:TPU:120 now
where the time goes in v3:
time: 102 us
  Pallas kernels  98 us (96%)
  local copies, waits for them, and re-layouts  3.08 us (3%)
    pallas_call x1, Pallas kernels, shards(): pl.pallas_call(layer_kernel, in_specs=[here] * 6, out_specs=here, out_sha...  98 us
    unnamed x1, local copies, waits for them, and re-layouts  2.29 us

profile of v3, /device:TPU:120, one launch (start us, length us, event | category | flops | bytes accessed | tf_op | source)
XLA Modules:
  0.0 101.8 jit_solution(15346339392090215988)
XLA Ops:
  0.0 0.7 convert_bitcast_fusion
  0.7 0.1 copy.8
  0.8 0.7 copy.9.beta_ref
  1.5 98.0 %shard_map.64 = bf16[128,4096]{1,0:T(8,128)(2,1)} custom-call(bf16[128,4096]{1,0:T(8,128)(2,1)} %q_ref.1, bf16[128,2,4096]{2,1,0:T(2,128)(2,1)} %k_ref.1, bf16[128,2,4096]{2,1,0:T(2,128)(2,1)} %v_ref.1, f32[16,1,256]{2,1,0:T(1,128)} %copy.9.beta_ref, bf16[128,4096]{1,0:T(8,128)(2,1)} %gate_ref.1, f32[1,256]{1,0:T(1,128)} %bitcast.5), custom_call_target="tpu_custom_call" | custom-call | tf_op jit(solution)/shard_map/pallas_call | solution.py:419
  99.5 2.3 %copy.11 = bf16[128,4096]{1,0:T(8,128)(2,1)} copy(bf16[128,4096]{1,0:T(8,128)(2,1)} %shard_map.64) | data formatting | bytes 2097152

commit v4 on v3

--- a/solution.py
+++ b/solution.py
@@ -114,23 +114,17 @@
         mask_ref[level] = jnp.where(inside, 1.0, 0.0).astype(bf16)
 
 
-def gated(o, gain, gate):
-    scale = lax.rsqrt(jnp.mean(o * o, axis=-1, keepdims=True) + EPS)
-    normed = (o * scale * gain).astype(bf16).astype(f32)
-    gate = gate.astype(f32)
-    return (normed * (gate / (1.0 + jnp.exp(-gate)))).astype(bf16)
-
-
 def put_pair(ref, values):
     ref[0], ref[1] = split(values)
 
 
 def layer_kernel(
-    q_ref, k_ref, v_ref, beta_ref, gate_ref, gain_ref, out_ref,
-    mask, wy, blk, x_out, x_in, pxa, pxb, y_out, y_in, pya, pyb, z_in, z_out, u_out, u_in,
+    q_hbm, k_hbm, v_hbm, beta_ref, gain_ref, out_ref,
+    q_ref, k_ref, v_ref, beta, mask, wy, blk, x_out, x_in, pxa, pxb, y_out, y_in, pf_out, pf_in, line, line_in,
+    z_in, z_mid, z_out, u_in,
     s_out, s_in, mine, c_out, c_in,
-    core_send, core_recv, x_send, x_recv, y_send, y_recv, z_send, z_recv, u_send, u_recv, s_send, s_recv,
-    c_send, c_recv, here,
+    core_send, core_recv, x_send, x_recv, y_send, y_recv, z_send, z_recv, p_send, p_recv, u_send, u_recv, s_send, s_recv,
+    c_send, c_recv, q_here, k_here, v_here,
 ):
     z, y, x, c = (lax.axis_index(name) for name in AXES)
     other = {"core": 1 - c}
@@ -140,7 +134,7 @@
 
     barrier = pltpu.get_barrier_semaphore()
     greeted = [other] + [along("x", x, o) for o in (1, 2, 3)] + [along("y", y, o) for o in (1, 2, 3)]
-    greeted += [along("z", z, o) for o in (1, 3)]
+    greeted += [along("z", z, o) for o in (1, 2, 3)]
     for device in greeted:
         pl.semaphore_signal(barrier, inc=1, device_id=device, device_id_type=MESH)
 
@@ -160,11 +154,20 @@
     def y_copy(i, source, root):
         return remote(y_out.at[i], y_in.at[source], y_send.at[i], y_recv.at[source], {"y": root})
 
-    def z_copy():
-        return remote(z_out, z_in, z_send.at[0], z_recv.at[0], along("z", z, 1))
+    def z_next(source):
+        return remote(source, z_in, z_send.at[0], z_recv.at[0], along("z", z, 1))
+
+    def z_skip():
+        return remote(z_out, z_mid, z_send.at[1], z_recv.at[1], along("z", z, 2))
+
+    def line_copy():
+        return remote(line, line_in, z_send.at[2], z_recv.at[2], along("z", z, 1))
+
+    def p_copy(i, o, dest):
+        return remote(pf_out.at[dest], pf_in.at[i], p_send.at[o], p_recv.at[i], {"y": dest})
 
     def u_copy(i, o, dest):
-        return remote(u_out.at[dest], u_in.at[i], u_send.at[o], u_recv.at[i], {"y": dest})
+        return remote(z_in, u_in.at[i], u_send.at[o], u_recv.at[i], {"y": dest})
 
     def s_copy(i, o, dest, source):
         j = 2 * source + i
@@ -176,57 +179,99 @@
     def lanes_of(head):
         return pl.ds(pl.multiple_of(head * DK, DK), DK)
 
+    def load(head):
+        lanes = lanes_of(head)
+        return (
+            pltpu.make_async_copy(k_hbm.at[:, :, lanes], k_ref.at[:, :, lanes], k_here.at[head]),
+            pltpu.make_async_copy(v_hbm.at[:, :, lanes], v_ref.at[:, :, lanes], v_here.at[head]),
+        )
+
+    def place(own, j):
+        return own * c + (1 - own) * 2, 8 * (own * c + (1 - own) * (1 - c)) + j
+
+    def away(p):
+        own = p % 2
+        return [(own, 2 * lax.rem(x + o, 4) + p // 2) for o in (1, 3, 2)]
+
+    near = [(own, 2 * x + i) for own in (0, 1) for i in (0, 1)]
+
+    def start_loads(group):
+        for own, j in group:
+            for copy in load(place(own, j)[1]):
+                copy.start()
+
+    def loads_of(p, carry):
+        start_loads(away(p))
+        return carry
+
+    lax.fori_loop(0, 4, loads_of, 0)
+    start_loads(near)
+    q_load = pltpu.make_async_copy(q_hbm, q_ref, q_here.at[0])
+    q_load.start()
+
     make_masks(mask)
-
-    def phase(p, carry):
-        i, own = p // 2, p % 2
-        group = own * c + (1 - own) * (1 - c)
-        slot = own * c + (1 - own) * 2
-        heads = [8 * group + 2 * n + i for n in range(4)]
-        lanes = [lanes_of(h) for h in heads]
-        a, b, w, y = factors(
+    token = lax.broadcasted_iota(jnp.int32, (CT, STEPS), 0)
+    step_of = lax.broadcasted_iota(jnp.int32, (CT, STEPS), 1)
+    spread = [jnp.where(step_of == 2 * token + r, 1.0, 0.0).astype(bf16) for r in (0, 1)]
+    beta[...] = mm(beta_ref[0], spread[0]) + mm(beta_ref[1], spread[1])
+
+    def make_pairs(group):
+        places = [place(own, j) for own, j in group]
+        for slot, head in places:
+            for copy in load(head):
+                copy.wait()
+        lanes = [lanes_of(head) for slot, head in places]
+        a, b, w, y_rows = factors(
             [k_ref[:, :, n].reshape(STEPS, DK) for n in lanes],
             [v_ref[:, :, n].reshape(STEPS, DK) for n in lanes],
-            [beta_ref[h] for h in heads],
+            [beta[pl.ds(head, 1), :] for slot, head in places],
             mask,
         )
-        for n in range(4):
-            j = 2 * n + i
+        for n, (slot, head) in enumerate(places):
+            j = group[n][1]
             put_pair(blk.at[slot, j, pl.ds(0, 2)], a[n])
             put_pair(blk.at[slot, j, pl.ds(2, 2)], b[n])
-            wy[heads[n], 0], wy[heads[n], 1] = w[n]
-            wy[heads[n], 2], wy[heads[n], 3] = y[n]
+            wy[head, 0], wy[head, 1] = w[n]
+            wy[head, 2], wy[head, 3] = y_rows[n]
+
+    def merge(j, pair):
+        core_copy(j, 1 - c).wait_recv()
+        later = (blk[1, j, 0], blk[1, j, 1])
+        put_pair(pair.at[pl.ds(0, 2)], mm_both(later, (blk[0, j, 0], blk[0, j, 1])))
+        pair[2] = (
+            mm_both(later, (blk[0, j, 2], blk[0, j, 3]))
+            + blk[1, j, 2].astype(f32)
+            + blk[1, j, 3].astype(f32)
+        ).astype(bf16)
+
+    def phase(p, carry):
+        i = p // 2
+        group = away(p)
+        make_pairs(group)
 
         @pl.when(p == 0)
         def _():
             pl.semaphore_wait(barrier, len(greeted))
 
-        @pl.when(own == 0)
-        def _():
-            for n in range(4):
-                core_copy(2 * n + i, c).start()
-
-        @pl.when(own == 1)
-        def _():
-            for o in (1, 3, 2, 0):
-                dest = lax.rem(x + o, 4)
-                j = 2 * dest + i
-                core_copy(j, 1 - c).wait_recv()
-                later = (blk[1, j, 0], blk[1, j, 1])
-                put_pair(x_out.at[j, pl.ds(0, 2)], mm_both(later, (blk[0, j, 0], blk[0, j, 1])))
-                x_out[j, 2] = (
-                    mm_both(later, (blk[0, j, 2], blk[0, j, 3]))
-                    + blk[1, j, 2].astype(f32)
-                    + blk[1, j, 3].astype(f32)
-                ).astype(bf16)
-                if o:
-                    x_copy(i, o, j, x).start()
-                else:
-                    pltpu.make_async_copy(x_out.at[j], x_in.at[x, i], here.at[i]).start()
+        @pl.when(p % 2 == 0)
+        def _():
+            for own, j in group:
+                core_copy(j, c).start()
+
+        @pl.when(p % 2 == 1)
+        def _():
+            for o in (1, 3, 2):
+                j = 2 * lax.rem(x + o, 4) + i
+                merge(j, x_out.at[j])
+                x_copy(i, o, j, x).start()
 
         return carry
 
     lax.fori_loop(0, 4, phase, 0)
+    make_pairs(near)
+    for i in (0, 1):
+        core_copy(2 * x + i, c).start()
+    q_load.wait()
 
     def answer(p, carry):
         heads = [4 * p + n for n in range(4)]
@@ -244,40 +289,52 @@
         return carry
 
     lax.fori_loop(0, 4, answer, 0)
-
-    def compose(pairs, pa, pb):
+    for i in (0, 1):
+        merge(2 * x + i, x_in.at[x, i])
+
+    def compose(pairs, whole, prefix):
+        p = [(pairs[n, 0], pairs[n, 1]) for n in range(4)]
+        b = [pairs[n, 2] for n in range(4)]
+        a10, a32 = split(mm_both(p[1], p[0])), split(mm_both(p[3], p[2]))
+        b10 = mm(p[1][0], b[0]) + mm(p[1][1], b[0]) + b[1].astype(f32)
+        b32 = mm(p[3][0], b[2]) + mm(p[3][1], b[2]) + b[3].astype(f32)
+        b10s = split(b10)
+        whole(split(mm_both(a32, a10)), mm_both(a32, b10s) + b32)
+        prefix(1, p[0], b[0].astype(f32))
+        prefix(2, a10, b10)
+        prefix(3, split(mm_both(p[2], a10)), mm_both(p[2], b10s) + b[2].astype(f32))
+
+    def identity():
         eye = lax.broadcasted_iota(jnp.int32, (DK, DK), 0) == lax.broadcasted_iota(jnp.int32, (DK, DK), 1)
-        pa[0, 0] = jnp.where(eye, 1.0, 0.0).astype(bf16)
-        pa[0, 1] = jnp.zeros((DK, DK), bf16)
-        pb[0] = jnp.zeros((DK, DK), f32)
-        a = (pairs[0, 0], pairs[0, 1])
-        b = pairs[0, 2].astype(f32)
-        for n in range(1, 4):
-            pa[n, 0], pa[n, 1] = a
-            pb[n] = b
-            later = (pairs[n, 0], pairs[n, 1])
-            a = split(mm_both(later, a))
-            b = mm_both(later, split(b)) + pairs[n, 2].astype(f32)
-        return a, b
+        return jnp.where(eye, 1.0, 0.0).astype(bf16), jnp.zeros((DK, DK), bf16)
+
+    for i in (0, 1):
+        pxa[i, 0, 0], pxa[i, 0, 1] = identity()
+        pxb[i, 0] = jnp.zeros((DK, DK), f32)
 
     def over_x(i):
-        pltpu.make_async_copy(x_out.at[2 * x + i], x_in.at[x, i], here.at[i]).wait()
         for o in (1, 3, 2):
             source = lax.rem(x + o, 4)
             x_copy(i, o, 2 * source + i, source).wait_recv()
-        a, b = compose(x_in.at[:, i], pxa.at[i], pxb.at[i])
         root = 2 * c + i
 
-        @pl.when(y == root)
-        def _():
-            y_in[y, 0], y_in[y, 1] = a
-            y_in[y, 2] = b.astype(bf16)
-
-        @pl.when(y != root)
-        def _():
-            y_out[i, 0], y_out[i, 1] = a
-            y_out[i, 2] = b.astype(bf16)
-            y_copy(i, y, root).start()
+        def whole(a, b):
+            @pl.when(y == root)
+            def _():
+                y_in[y, 0], y_in[y, 1] = a
+                y_in[y, 2] = b.astype(bf16)
+
+            @pl.when(y != root)
+            def _():
+                y_out[i, 0], y_out[i, 1] = a
+                y_out[i, 2] = b.astype(bf16)
+                y_copy(i, y, root).start()
+
+        def prefix(n, a, b):
+            pxa[i, n, 0], pxa[i, n, 1] = a
+            pxb[i, n] = b
+
+        compose(x_in.at[:, i], whole, prefix)
 
     i_root = y % 2
     is_root = y // 2 == c
@@ -285,42 +342,84 @@
     def over_y():
         for o in (1, 3, 2):
             y_copy(i_root, lax.rem(y + o, 4), y).wait_recv()
-        a, b = compose(y_in, pya, pyb)
-        z_out[...] = b.astype(bf16)
-        pya[4, 0], pya[4, 1] = a
-        pyb[4] = b
+
+        def whole(a, b):
+            line[0], line[1] = a
+            line[2], line[3] = split(b)
+
+            @pl.when(z == 0)
+            def _():
+                z_next(line.at[2]).start()
+
+            @pl.when(z == 2)
+            def _():
+                line_copy().start()
+
+        def prefix(n, a, b):
+            pf_out[n, 0], pf_out[n, 1] = a
+            pf_out[n, 2], pf_out[n, 3] = split(b)
+
+        compose(y_in, whole, prefix)
+        for o in (1, 2, 3):
+            dest = lax.rem(y + o, 4)
+
+            @pl.when(dest > 0)
+            def _():
+                p_copy(i_root, o, dest).start()
+
+        @pl.when(y > 0)
+        def _():
+            for n in range(4):
+                pf_in[i_root, n] = pf_out[y, n]
+
+    def advance(pair, s):
+        out = mm(pair[0], s) + mm(pair[1], s)
+        return out + pair[2].astype(f32) + pair[3].astype(f32)
 
     def over_z():
         @pl.when(z == 0)
         def _():
             z_in[...] = jnp.zeros((DK, DK), bf16)
 
-        @pl.when(z > 0)
-        def _():
-            z_copy().wait_recv()
-            z_out[...] = (mm(pya[4, 0], z_in[...]) + mm(pya[4, 1], z_in[...]) + pyb[4]).astype(bf16)
-
-        @pl.when(z < 3)
-        def _():
-            z_copy().start()
-
-        for o in (1, 3, 2, 0):
-            dest = lax.rem(y + o, 4)
-            now = mm(pya[dest, 0], z_in[...]) + mm(pya[dest, 1], z_in[...]) + pyb[dest]
-            if o:
-                put_pair(u_out.at[dest], now)
-                u_copy(i_root, o, dest).start()
-            else:
-                put_pair(u_in.at[i_root], now)
+        @pl.when(z == 1)
+        def _():
+            z_next(z_out).wait_recv()
+            z_out[...] = advance(line, z_in[...]).astype(bf16)
+            z_skip().start()
+            z_next(z_out).start()
+
+        @pl.when(z == 2)
+        def _():
+            z_next(z_out).wait_recv()
+
+        @pl.when(z == 3)
+        def _():
+            line_copy().wait_recv()
+            z_skip().wait_recv()
+            z_in[...] = advance(line_in, z_mid[...]).astype(bf16)
+
+        for o in (2, 1, 3):
+            u_copy(i_root, o, lax.rem(y + o, 4)).start()
+        u_in[i_root] = z_in[...]
 
     def down(i):
         root = 2 * c + i
 
+        @pl.when(y == 0)
+        def _():
+            pf_in[i, 0], pf_in[i, 1] = identity()
+            pf_in[i, 2] = jnp.zeros((DK, DK), bf16)
+            pf_in[i, 3] = jnp.zeros((DK, DK), bf16)
+
+        @pl.when((y != root) & (y > 0))
+        def _():
+            p_copy(i, 1, y).wait_recv()
+
         @pl.when(y != root)
         def _():
             u_copy(i, 1, y).wait_recv()
 
-        s = (u_in[i, 0], u_in[i, 1])
+        s = split(advance(pf_in.at[i], u_in[i]))
         for o in (1, 3, 2, 0):
             dest = lax.rem(x + o, 4)
             now = (mm_both((pxa[i, dest, 0], pxa[i, dest, 1]), s) + pxb[i, dest]).astype(bf16)
@@ -365,8 +464,8 @@
     def finish(head, state):
         o = mm(wy[head, 0, :CT], state) + mm(wy[head, 0, CT:], state)
         o += wy[head, 1, :CT].astype(f32) + wy[head, 1, CT:].astype(f32)
-        lanes = lanes_of(head)
-        out_ref[:, lanes] = gated(o, gain_ref[...], gate_ref[:, lanes])
+        scale = lax.rsqrt(jnp.mean(o * o, axis=-1, keepdims=True) + EPS)
+        out_ref[:, lanes_of(head)] = (o * scale * gain_ref[...]).astype(bf16)
 
     def last_own(j, carry):
         finish(8 * c + j, mine[j])
@@ -403,25 +502,42 @@
     @pl.when(is_root)
     def _():
         for o in (1, 2, 3):
-            u_copy(i_root, o, lax.rem(y + o, 4)).wait_send()
-
-        @pl.when(z < 3)
-        def _():
-            z_copy().wait_send()
+            dest = lax.rem(y + o, 4)
+            u_copy(i_root, o, dest).wait_send()
+
+            @pl.when(dest > 0)
+            def _():
+                p_copy(i_root, o, dest).wait_send()
+
+        @pl.when(z < 2)
+        def _():
+            z_next(z_out).wait_send()
+
+        @pl.when(z == 1)
+        def _():
+            z_skip().wait_send()
+
+        @pl.when(z == 2)
+        def _():
+            line_copy().wait_send()
 
 
 def shards(queries, keys, values, betas, gate, norm_gain):
-    beta_rows = betas.astype(f32).transpose(2, 0, 1).reshape(H, 1, STEPS)
     here = pl.BlockSpec(memory_space=pltpu.VMEM)
+    outside = pl.BlockSpec(memory_space=pl.ANY)
     vm = pltpu.VMEM
     dma = pltpu.SemaphoreType.DMA
     tile = (DK, DK)
-    return pl.pallas_call(
+    normed = pl.pallas_call(
         layer_kernel,
-        in_specs=[here] * 6,
+        in_specs=[outside] * 3 + [here] * 2,
         out_specs=here,
         out_shape=jax.ShapeDtypeStruct((CT, H * DK), bf16),
         scratch_shapes=[
+            vm((CT, H * DK), bf16),
+            vm((CT, 2, H * DK), bf16),
+            vm((CT, 2, H * DK), bf16),
+            vm((H, STEPS), f32),
             vm((LEVELS - 1, HALF, HALF), bf16),
             vm((H, 4) + tile, bf16),
             vm((3, 8, 4) + tile, bf16),
@@ -431,12 +547,14 @@
             vm((2, 4) + tile, f32),
             vm((2, 3) + tile, bf16),
             vm((4, 3) + tile, bf16),
-            vm((5, 2) + tile, bf16),
-            vm((5,) + tile, f32),
+            vm((4, 4) + tile, bf16),
+            vm((2, 4) + tile, bf16),
+            vm((4,) + tile, bf16),
+            vm((4,) + tile, bf16),
             vm(tile, bf16),
             vm(tile, bf16),
-            vm((4, 2) + tile, bf16),
-            vm((2, 2) + tile, bf16),
+            vm(tile, bf16),
+            vm((2,) + tile, bf16),
             vm((4, 2) + tile, bf16),
             vm((8,) + tile, bf16),
             vm((8,) + tile, bf16),
@@ -448,20 +566,26 @@
             dma((4, 2)),
             dma((2,)),
             dma((4,)),
-            dma((1,)),
-            dma((1,)),
+            dma((3,)),
+            dma((3,)),
+            dma((4,)),
+            dma((2,)),
             dma((4,)),
             dma((2,)),
             dma((4, 2)),
             dma((8,)),
             dma((8,)),
             dma((8,)),
-            dma((2,)),
+            dma((1,)),
+            dma((H,)),
+            dma((H,)),
         ],
         compiler_params=pltpu.CompilerParams(
             collective_id=0, has_side_effects=True, vmem_limit_bytes=60 << 20
         ),
-    )(queries, keys, values, beta_rows, gate, norm_gain.reshape(1, DK))
+    )(queries, keys, values, betas.transpose(1, 2, 0), norm_gain.reshape(1, DK))
+    gate = gate.astype(f32)
+    return (normed.astype(f32) * (gate / (1.0 + jnp.exp(-gate)))).astype(bf16)
 
 
 def solution(mesh):

time: 102 us -> 95.7 us (0.938)
  the two profiles are of different devices: /device:TPU:120 before, /device:TPU:96 now
where the time goes in v4:
time: 95.7 us; the launch traced here: 95.3 us
  Pallas kernels  92.4 us (97%)
  other arithmetic  2.83 us (3%)
    pallas_call x1, Pallas kernels, shards(): pl.pallas_call(layer_kernel, in_specs=[outside] * 3 + [here] * 2, out_spe...  92.4 us
    convert_element_type x1, other arithmetic, shards(): return (normed.astype(f32) * (gate / (1.0 + jnp.exp(-gate)))).astype(bf16)  2.83 us

profile of v4, /device:TPU:96, one launch (start us, length us, event | category | flops | bytes accessed | tf_op | source)
XLA Modules:
  0.0 95.3 jit_solution(15195487567147798991)
XLA Ops:
  0.0 0.0 copy-start
  0.0 92.4 %shard_map.64 = bf16[128,4096]{1,0:T(8,128)(2,1)} custom-call(bf16[128,4096]{1,0:T(8,128)(2,1)} %q_hbm.1, bf16[128,2,4096]{2,1,0:T(2,128)(2,1)} %k_hbm.1, bf16[128,2,4096]{2,1,0:T(2,128)(2,1)} %v_hbm.1, bf16[2,16,128]{2,1,0:T(8,128)(2,1)} %bitcast.2, f32[1,256]{1,0:T(1,128)} %bitcast.3), custom_call_target="tpu_custom_call" | custom-call | tf_op jit(solution)/shard_map/pallas_call | solution.py:531
  92.4 0.0 copy-done
  92.4 2.8 %fusion.3 = bf16[128,4096]{1,0:T(8,128)(2,1)} fusion(bf16[128,4096]{1,0:T(8,128)(2,1)S(1)} %copy-done, bf16[128,4096]{1,0:T(8,128)(2,1)} %shard_map.64), kind=kLoop, calls=%fused_computation.5 | loop fusion | flops 3670016 | bytes 3145728 | tf_op jit(solution)/shard_map/convert_element_type | solution.py:588
Async XLA Ops:
  0.0 92.4 %copy-start = (bf16[128,4096]{1,0:T(8,128)(2,1)S(1)}, bf16[128,4096]{1,0:T(8,128)(2,1)}, u32[]{:S(2)}) copy-start(bf16[128,4096]{1,0:T(8,128)(2,1)} %param.10) | copy-start | bytes 3145732

commit v5 on v4

--- a/solution.py
+++ b/solution.py
@@ -122,7 +122,7 @@
     q_hbm, k_hbm, v_hbm, beta_ref, gain_ref, out_ref,
     q_ref, k_ref, v_ref, beta, mask, wy, blk, x_out, x_in, pxa, pxb, y_out, y_in, pf_out, pf_in, line, line_in,
     z_in, z_mid, z_out, u_in,
-    s_out, s_in, mine, c_out, c_in,
+    s_out, s_in, c_out, c_in,
     core_send, core_recv, x_send, x_recv, y_send, y_recv, z_send, z_recv, p_send, p_recv, u_send, u_recv, s_send, s_recv,
     c_send, c_recv, q_here, k_here, v_here,
 ):
@@ -204,8 +204,9 @@
         start_loads(away(p))
         return carry
 
-    lax.fori_loop(0, 4, loads_of, 0)
+    lax.fori_loop(0, 2, loads_of, 0)
     start_loads(near)
+    lax.fori_loop(2, 4, loads_of, 0)
     q_load = pltpu.make_async_copy(q_hbm, q_ref, q_here.at[0])
     q_load.start()
 
@@ -265,13 +266,17 @@
                 merge(j, x_out.at[j])
                 x_copy(i, o, j, x).start()
 
+        @pl.when(p == 1)
+        def _():
+            make_pairs(near)
+            for i in (0, 1):
+                core_copy(2 * x + i, c).start()
+
         return carry
 
     lax.fori_loop(0, 4, phase, 0)
-    make_pairs(near)
     for i in (0, 1):
-        core_copy(2 * x + i, c).start()
-    q_load.wait()
+        merge(2 * x + i, x_in.at[x, i])
 
     def answer(p, carry):
         heads = [4 * p + n for n in range(4)]
@@ -288,9 +293,6 @@
             wy[h, 1, :CT], wy[h, 1, CT:] = split(o_now[n])
         return carry
 
-    lax.fori_loop(0, 4, answer, 0)
-    for i in (0, 1):
-        merge(2 * x + i, x_in.at[x, i])
 
     def compose(pairs, whole, prefix):
         p = [(pairs[n, 0], pairs[n, 1]) for n in range(4)]
@@ -432,6 +434,8 @@
     first_root = is_root & (i_root == 0)
     second_root = is_root & (i_root == 1)
     over_x(0)
+    q_load.wait()
+    lax.fori_loop(0, 4, answer, 0)
     pl.when(first_root)(over_y)
     over_x(1)
     pl.when(first_root)(over_z)
@@ -441,43 +445,32 @@
     pl.when(second_root & (z >= 2))(over_z)
     down(1)
 
-    def over_cores(i, carry):
+    def over_cores(i):
         for o in (0, 1, 3, 2):
             source = lax.rem(x + o, 4)
             j = 2 * source + i
             if o:
                 s_copy(i, o, source, source).wait_recv()
             first = s_in[j]
-            second = (
-                mm(blk[0, j, 0], first)
-                + mm(blk[0, j, 1], first)
-                + blk[0, j, 2].astype(f32)
-                + blk[0, j, 3].astype(f32)
-            ).astype(bf16)
-            mine[j] = jnp.where(c == 0, first, second)
+            second = advance(blk.at[0, j], first).astype(bf16)
             c_out[j] = jnp.where(c == 0, second, first)
             c_copy(j).start()
-        return carry
-
-    lax.fori_loop(0, 2, over_cores, 0)
-
-    def finish(head, state):
-        o = mm(wy[head, 0, :CT], state) + mm(wy[head, 0, CT:], state)
-        o += wy[head, 1, :CT].astype(f32) + wy[head, 1, CT:].astype(f32)
-        scale = lax.rsqrt(jnp.mean(o * o, axis=-1, keepdims=True) + EPS)
-        out_ref[:, lanes_of(head)] = (o * scale * gain_ref[...]).astype(bf16)
-
-    def last_own(j, carry):
-        finish(8 * c + j, mine[j])
-        return carry
-
-    def last_other(j, carry):
-        c_copy(j).wait_recv()
-        finish(8 * (1 - c) + j, c_in[j])
-        return carry
-
-    lax.fori_loop(0, 8, last_own, 0)
-    lax.fori_loop(0, 8, last_other, 0)
+            s_in[j] = jnp.where(c == 0, first, second)
+
+    def finish(heads, states):
+        o = [mm(wy[h, 0, :CT], s) + mm(wy[h, 0, CT:], s) for h, s in zip(heads, states)]
+        o = [x + wy[h, 1, :CT].astype(f32) + wy[h, 1, CT:].astype(f32) for h, x in zip(heads, o)]
+        scale = [lax.rsqrt(jnp.mean(x * x, axis=-1, keepdims=True) + EPS) for x in o]
+        for n, h in enumerate(heads):
+            out_ref[:, lanes_of(h)] = (o[n] * scale[n] * gain_ref[...]).astype(bf16)
+
+    for i in (0, 1):
+        over_cores(i)
+        js = [2 * n + i for n in range(4)]
+        finish([8 * c + j for j in js], [s_in[j] for j in js])
+        for j in js:
+            c_copy(j).wait_recv()
+        finish([8 * (1 - c) + j for j in js], [c_in[j] for j in js])
 
     def drain(j, carry):
         core_copy(j, c).wait_send()
@@ -559,7 +552,6 @@
             vm((8,) + tile, bf16),
             vm((8,) + tile, bf16),
             vm((8,) + tile, bf16),
-            vm((8,) + tile, bf16),
             dma((8,)),
             dma((8,)),
             dma((4, 2)),
@@ -581,7 +573,7 @@
             dma((H,)),
         ],
         compiler_params=pltpu.CompilerParams(
-            collective_id=0, has_side_effects=True, vmem_limit_bytes=60 << 20
+            collective_id=0, has_side_effects=True, vmem_limit_bytes=63 << 20
         ),
     )(queries, keys, values, betas.transpose(1, 2, 0), norm_gain.reshape(1, DK))
     gate = gate.astype(f32)

time: 95.7 us -> 93.2 us (0.974)
  Pallas kernels: 92.4 us -> 88.9 us
    pallas_call x1, Pallas kernels: 92.4 us -> 88.9 us  [shards(): pl.pallas_call(layer_kernel, in_specs=[outside] * 3 + [here] * 2, out_spe...]
where the time goes in v5:
time: 93.2 us; the launch traced here: 92 us
  Pallas kernels  88.9 us (95%)
  other arithmetic  3.15 us (3%)
    pallas_call x1, Pallas kernels, shards(): pl.pallas_call(layer_kernel, in_specs=[outside] * 3 + [here] * 2, out_spe...  88.9 us
    convert_element_type x1, other arithmetic, shards(): return (normed.astype(f32) * (gate / (1.0 + jnp.exp(-gate)))).astype(bf16)  3.15 us

profile of v5, /device:TPU:96, one launch (start us, length us, event | category | flops | bytes accessed | tf_op | source)
XLA Modules:
  0.0 92.0 jit_solution(14768450769703909661)
XLA Ops:
  0.0 88.9 %shard_map.64 = bf16[128,4096]{1,0:T(8,128)(2,1)} custom-call(bf16[128,4096]{1,0:T(8,128)(2,1)} %q_hbm.1, bf16[128,2,4096]{2,1,0:T(2,128)(2,1)} %k_hbm.1, bf16[128,2,4096]{2,1,0:T(2,128)(2,1)} %v_hbm.1, bf16[2,16,128]{2,1,0:T(8,128)(2,1)} %bitcast.2, f32[1,256]{1,0:T(1,128)} %bitcast.3), custom_call_target="tpu_custom_call" | custom-call | tf_op jit(solution)/shard_map/pallas_call | solution.py:524
  88.9 3.1 %fusion.3 = bf16[128,4096]{1,0:T(8,128)(2,1)} fusion(bf16[128,4096]{1,0:T(8,128)(2,1)} %param.10, bf16[128,4096]{1,0:T(8,128)(2,1)} %shard_map.64), kind=kLoop, calls=%fused_computation.5 | loop fusion | flops 3670016 | bytes 3145728 | tf_op jit(solution)/shard_map/convert_element_type | solution.py:580
